TPU v7x, 512 devices: a whole 4x4x16 slice. The times are simulated.
512 devices in a mesh: pb: 64 (over z_lo, x, core), vert: 8 (over z_hi, y).
Axes of the slice: x: 4, y: 4, z: 16 (z_hi: 2, z_lo: 8; z = z_hi * 8 + z_lo), core: 2. Of those that a mesh axis runs over, the one named last changes fastest.
Arguments:
- cholesky: bfloat16 [64, 64, 1, 2, 128, 128], P('pb', None, None, None, 'vert'), may hold values from -6 to 6
- trial_rows: bfloat16 [64, 2, 32, 128], P('pb'), may hold values from -0.5 to 0.5
- occupied: int32 [64], replicated, may hold values from 16 to 32
- kpoint_map: int32 [64, 64], replicated, may hold values from 0 to 63, as said below
- partner: int32 [64], replicated, may hold values from 0 to 63, as said below
Outputs:
- paired_plus: bfloat16 [64, 64, 1, 2, 32, 128], P('pb', None, None, None, 'vert')
- paired_minus: bfloat16 [64, 64, 1, 2, 32, 128], P('pb', None, None, None, 'vert')
Inputs may be any that keep to these rules, and one draw needn't show every extreme that they name: The k-points form a cyclic group of 64 elements labelled in an order drawn from the seed; kpoint_map[q, k] is the label of k - q, so kpoint_map[partner[q], kpoint_map[q, k]] = k. partner[q] is the label of -q in the same group; partner is an involution.
All inputs are finite; a program needn't handle non-finite values.
Results may differ from a plain program's by a relative error of at most 0.00165.
Values may be sent and summed in bfloat16 or wider, within the bound.
A program may use at most 64 MiB of HBM per device.

v0:
```python
import jax
import jax.numpy as jnp
from jax import lax
from jax.sharding import PartitionSpec as P


def rotate(orbitals, block, pattern, conjugate):
    trial_re = jnp.take(orbitals, 0, axis=-3)
    trial_im = jnp.take(orbitals, 1, axis=-3)
    block_re = block[:, :, 0]
    block_im = block[:, :, 1]

    def product(left, right):
        return jnp.einsum(pattern, left, right, preferred_element_type=jnp.float32)

    if conjugate:
        real_part = product(trial_re, block_re) + product(trial_im, block_im)
        imag_part = product(trial_im, block_re) - product(trial_re, block_im)
    else:
        real_part = product(trial_re, block_re) - product(trial_im, block_im)
        imag_part = product(trial_re, block_im) + product(trial_im, block_re)
    return jnp.stack([real_part, imag_part], axis=2)


def combine(own_term, mirror_term):
    plus_part = ((own_term + mirror_term) * 0.5).astype(jnp.bfloat16)
    difference = own_term - mirror_term
    minus_part = (jnp.stack([difference[:, :, 1], -difference[:, :, 0]], axis=2) * 0.5).astype(
        jnp.bfloat16
    )
    return (plus_part, minus_part)


def local(cholesky, trial_rows, occupied, kpoint_map, partner):
    own_blk = cholesky[0]
    source = lax.axis_index("pb")
    order_rows = kpoint_map[partner[source]]
    ready_blk = jnp.take(own_blk, order_rows, axis=0)
    mirror_blk = lax.all_to_all(ready_blk, "vert", split_axis=4, concat_axis=3, tiled=True)
    occ_width = trial_rows.shape[2]
    gathered = lax.all_gather(trial_rows, "pb", axis=0, tiled=True)
    live_rows = jnp.arange(occ_width, dtype=jnp.int32)[None, :] < occupied[:, None]
    masked = jnp.where(live_rows[:, None, :, None], gathered, jnp.zeros_like(gathered))
    own_out = rotate(masked, own_blk, "kar,kgsr->kgas", False)
    mirror_out = rotate(masked, mirror_blk, "kau,kgus->kgas", True)
    own_term, mirror_term = (
        lax.all_to_all(own_out, "pb", split_axis=0, concat_axis=0, tiled=True),
        lax.all_to_all(mirror_out, "pb", split_axis=0, concat_axis=0, tiled=True),
    )
    mirror_term = jnp.take(mirror_term, partner, axis=0)
    plus_part, minus_part = combine(own_term, mirror_term)
    plus_part, minus_part = (
        lax.all_to_all(plus_part, "vert", split_axis=3, concat_axis=4, tiled=True),
        lax.all_to_all(minus_part, "vert", split_axis=3, concat_axis=4, tiled=True),
    )
    return (plus_part[None], minus_part[None])


def solution(mesh):
    in_specs = (P("pb", None, None, None, "vert", None), P("pb", None, None, None), P(), P(), P())
    out_specs = (P("pb", None, None, None, "vert", None), P("pb", None, None, None, "vert", None))
    return jax.shard_map(local, mesh=mesh, in_specs=in_specs, out_specs=out_specs, check_vma=False)
```

profile of v0, /device:TPU:1, one launch (start us, length us, event | category | flops | bytes accessed | tf_op | source)
XLA Modules:
  0.0 269.7 jit_solution(15749275120193534057)
XLA Ops:
  7.2 1.2 dynamic_slice.6
  10.4 0.7 fusion.14
  11.1 0.7 compare_and_fusion
  11.8 1.7 gather_fusion
  13.6 1.7 copy.80
  15.3 1.5 reshape.234
  16.9 18.3 %all-to-all-start.1 = ((bf16[8,2,16384]{2,1,0:T(2,128)(2,1)}), bf16[8,2,16384]{2,1,0:T(2,128)(2,1)S(1)}, u32[]{:S(2)}, u32[]{:S(2)}) async-start(bf16[8,2,16384]{2,1,0:T(2,128)(2,1)} %reshape.234), calls=%async_computation.1 | async-start | bytes 1048576 | tf_op jit(solution)/shard_map/all_to_all | solution.py:39
  35.2 0.7 all-gather.2.cloned.1.call-update
  35.9 16.3 %all-to-all-done.1 = bf16[8,2,16384]{2,1,0:T(2,128)(2,1)S(1)} async-done(((bf16[8,2,16384]{2,1,0:T(2,128)(2,1)}), bf16[8,2,16384]{2,1,0:T(2,128)(2,1)S(1)}, u32[]{:S(2)}, u32[]{:S(2)}) %all-to-all-start.1) | async-done | bytes 524320 | tf_op jit(solution)/shard_map/all_to_all | solution.py:39
  52.2 0.7 reshape.235
  54.3 0.6 copy.98
  54.9 106.1 %all-gather.2.cloned.1.call-done = bf16[64,2,32,128]{3,2,0,1:T(8,128)(2,1)} async-done(((bf16[1,2,32,128]{3,2,0,1:T(8,128)(2,1)}), bf16[64,2,32,128]{3,2,0,1:T(8,128)(2,1)}) %all-gather.2.cloned.1.call-update) | async-done | bytes 1048592 | tf_op jit(solution)/shard_map/all_gather | solution.py:41
  161.0 1.5 broadcast_select_fusion
  164.2 1.2 reshape.236
  165.3 8.8 %all-to-all-start.2 = ((f32[64,1,1024]{2,1,0:T(1,128)}), f32[64,1,1024]{2,1,0:T(1,128)S(1)}, u32[]{:S(2)}, u32[]{:S(2)}) async-start(f32[64,1,1024]{2,1,0:T(1,128)} %reshape.236), calls=%async_computation.2 | async-start | bytes 524288 | tf_op jit(solution)/shard_map/all_to_all | solution.py:48
  175.9 1.1 reshape.232
  177.0 17.0 %all-to-all-done.2 = f32[64,1,1024]{2,1,0:T(1,128)S(1)} async-done(((f32[64,1,1024]{2,1,0:T(1,128)}), f32[64,1,1024]{2,1,0:T(1,128)S(1)}, u32[]{:S(2)}, u32[]{:S(2)}) %all-to-all-start.2) | async-done | bytes 262176 | tf_op jit(solution)/shard_map/all_to_all | solution.py:48
  194.0 5.9 %all-to-all-start = ((f32[64,1,1024]{2,1,0:T(1,128)}), f32[64,1,1024]{2,1,0:T(1,128)S(1)}, u32[]{:S(2)}, u32[]{:S(2)}) async-start(f32[64,1,1024]{2,1,0:T(1,128)} %reshape.232), calls=%async_computation | async-start | bytes 524288 | tf_op jit(solution)/shard_map/all_to_all | solution.py:47
  200.5 1.3 reduce.1
  202.2 0.6 gather_fusion.1
  202.8 0.7 copy.86
  203.6 16.2 %all-to-all-done = f32[64,1,1024]{2,1,0:T(1,128)S(1)} async-done(((f32[64,1,1024]{2,1,0:T(1,128)}), f32[64,1,1024]{2,1,0:T(1,128)S(1)}, u32[]{:S(2)}, u32[]{:S(2)}) %all-to-all-start) | async-done | bytes 262176 | tf_op jit(solution)/shard_map/all_to_all | solution.py:47
  219.8 1.3 reduce
  221.4 0.7 copy.87
  222.4 0.9 reshape.240
  223.3 6.8 %all-to-all-start.4 = ((bf16[8,2,4096]{2,1,0:T(2,128)(2,1)}), bf16[8,2,4096]{2,1,0:T(2,128)(2,1)S(1)}, u32[]{:S(2)}, u32[]{:S(2)}) async-start(bf16[8,2,4096]{2,1,0:T(2,128)(2,1)} %reshape.240), calls=%async_computation.4 | async-start | bytes 262144 | tf_op jit(solution)/shard_map/all_to_all | solution.py:54
  230.1 0.9 reshape.238
  231.0 13.2 %all-to-all-done.4 = bf16[8,2,4096]{2,1,0:T(2,128)(2,1)S(1)} async-done(((bf16[8,2,4096]{2,1,0:T(2,128)(2,1)}), bf16[8,2,4096]{2,1,0:T(2,128)(2,1)S(1)}, u32[]{:S(2)}, u32[]{:S(2)}) %all-to-all-start.4) | async-done | bytes 131104 | tf_op jit(solution)/shard_map/all_to_all | solution.py:54
  244.2 3.4 %all-to-all-start.3 = ((bf16[8,2,4096]{2,1,0:T(2,128)(2,1)}), bf16[8,2,4096]{2,1,0:T(2,128)(2,1)S(1)}, u32[]{:S(2)}, u32[]{:S(2)}) async-start(bf16[8,2,4096]{2,1,0:T(2,128)(2,1)} %reshape.238), calls=%async_computation.3 | async-start | bytes 262144 | tf_op jit(solution)/shard_map/all_to_all | solution.py:53
  247.9 0.8 copy.96
  248.7 13.0 %all-to-all-done.3 = bf16[8,2,4096]{2,1,0:T(2,128)(2,1)S(1)} async-done(((bf16[8,2,4096]{2,1,0:T(2,128)(2,1)}), bf16[8,2,4096]{2,1,0:T(2,128)(2,1)S(1)}, u32[]{:S(2)}, u32[]{:S(2)}) %all-to-all-start.3) | async-done | bytes 131104 | tf_op jit(solution)/shard_map/all_to_all | solution.py:53
  262.0 0.8 copy.95
  (42 shorter events, 7.1 us)
Async XLA Ops:
  15.3 20.6 %copy-start.1 = (s32[64]{0:T(128)S(1)}, s32[64]{0:T(128)}, u32[]{:S(2)}) copy-start(s32[64]{0:T(128)} %param.11) | copy-start | bytes 772
  16.9 35.4 %all-to-all-start.1 = ((bf16[8,2,16384]{2,1,0:T(2,128)(2,1)}), bf16[8,2,16384]{2,1,0:T(2,128)(2,1)S(1)}, u32[]{:S(2)}, u32[]{:S(2)}) async-start(bf16[8,2,16384]{2,1,0:T(2,128)(2,1)} %reshape.234), calls=%async_computation.1 | async-start | bytes 1048576 | tf_op jit(solution)/shard_map/all_to_all | solution.py:39
  35.1 125.9 %all-gather.2.cloned.1.call-start = ((), (), s32[]{:S(2)}) async-start(), calls=%async_computation.5 | async-start | bytes 1064960 | tf_op jit(solution)/shard_map/all_gather | solution.py:41
  164.2 10.0 %copy-start = (bf16[1,64,1,2,16,128]{5,4,3,2,1,0:T(8,128)(2,1)S(1)}, bf16[1,64,1,2,16,128]{5,4,3,2,1,0:T(8,128)(2,1)}, u32[]{:S(2)}) copy-start(bf16[1,64,1,2,16,128]{5,4,3,2,1,0:T(8,128)(2,1)} %param.9) | copy-start | bytes 1572868
  165.3 28.7 %all-to-all-start.2 = ((f32[64,1,1024]{2,1,0:T(1,128)}), f32[64,1,1024]{2,1,0:T(1,128)S(1)}, u32[]{:S(2)}, u32[]{:S(2)}) async-start(f32[64,1,1024]{2,1,0:T(1,128)} %reshape.236), calls=%async_computation.2 | async-start | bytes 524288 | tf_op jit(solution)/shard_map/all_to_all | solution.py:48
  175.9 24.1 %copy-start.2 = (s32[64]{0:T(128)S(1)}, s32[64]{0:T(128)}, u32[]{:S(2)}) copy-start(s32[64]{0:T(128)} %param.13) | copy-start | bytes 772
  194.0 25.8 %all-to-all-start = ((f32[64,1,1024]{2,1,0:T(1,128)}), f32[64,1,1024]{2,1,0:T(1,128)S(1)}, u32[]{:S(2)}, u32[]{:S(2)}) async-start(f32[64,1,1024]{2,1,0:T(1,128)} %reshape.232), calls=%async_computation | async-start | bytes 524288 | tf_op jit(solution)/shard_map/all_to_all | solution.py:47
  223.3 21.0 %all-to-all-start.4 = ((bf16[8,2,4096]{2,1,0:T(2,128)(2,1)}), bf16[8,2,4096]{2,1,0:T(2,128)(2,1)S(1)}, u32[]{:S(2)}, u32[]{:S(2)}) async-start(bf16[8,2,4096]{2,1,0:T(2,128)(2,1)} %reshape.240), calls=%async_computation.4 | async-start | bytes 262144 | tf_op jit(solution)/shard_map/all_to_all | solution.py:54
  244.2 17.5 %all-to-all-start.3 = ((bf16[8,2,4096]{2,1,0:T(2,128)(2,1)}), bf16[8,2,4096]{2,1,0:T(2,128)(2,1)S(1)}, u32[]{:S(2)}, u32[]{:S(2)}) async-start(bf16[8,2,4096]{2,1,0:T(2,128)(2,1)} %reshape.238), calls=%async_computation.3 | async-start | bytes 262144 | tf_op jit(solution)/shard_map/all_to_all | solution.py:53
Sparse Core Ops, SparseCore 0:
  38.1 122.8 all-gather.1
where the time goes:
time: 275 us; the launch traced here: 270 us
  waiting for transfers between devices  182 us (66%)
  starting transfers between devices  43.2 us (16%)
  local copies, waits for them, and re-layouts  18.5 us (7%)
  between operations  16.3 us (6%)
  other arithmetic  6.02 us (2%)
  matrix products  3.15 us (1%)
    all_gather x1, waiting for transfers between devices, local(): gathered = lax.all_gather(trial_rows, 'pb', axis=0, tiled=True)  106 us
    all_to_all x1, starting transfers between devices, local(): lax.all_to_all(ready_blk, 'vert', split_axis=4, concat_axis=3, tiled=True)  18.3 us
    all_to_all x1, waiting for transfers between devices, local(): lax.all_to_all(mirror_out, 'pb', split_axis=0, concat_axis=0, tiled=True)  17 us
    all_to_all x1, waiting for transfers between devices, local(): lax.all_to_all(ready_blk, 'vert', split_axis=4, concat_axis=3, tiled=True)  16.3 us
    all_to_all x1, waiting for transfers between devices, local(): lax.all_to_all(own_out, 'pb', split_axis=0, concat_axis=0, tiled=True)  16.2 us
    all_to_all x1, waiting for transfers between devices, local(): lax.all_to_all(minus_part, 'vert', split_axis=3, concat_axis=4, tiled=True)  13.2 us
    all_to_all x1, waiting for transfers between devices, local(): lax.all_to_all(plus_part, 'vert', split_axis=3, concat_axis=4, tiled=True)  13 us
    unnamed x21, local copies, waits for them, and re-layouts  10.2 us
  transfers between devices with their start and end apart: 6, of which 6 were waited for; matrix products, arithmetic and copies ran while one was open for 4% of the time, Pallas kernels for 0%

commit v1 on v0

v1 whole, which is shorter than its diff:
```python
import functools

import jax
import jax.numpy as jnp
from jax import lax
from jax.experimental import pallas as pl
from jax.experimental.pallas import tpu as pltpu
from jax.sharding import PartitionSpec as P

MESH = pl.DeviceIdType.MESH
BITS = 19
TOP = 2**BITS - 1
BIAS = 128


def kpoint(jp, cp, y):
    return jp * 8 + ((y - jp + 8) % 4) * 2 + cp


def encode(own, real, imag):
    peak = jnp.maximum(jnp.maximum(jnp.abs(own), jnp.abs(real)), jnp.abs(imag))
    peak = jnp.max(peak, axis=0, keepdims=True)
    power = jnp.floor(jnp.log2(jnp.maximum(peak, 2.0**-100))) + 1.0
    scale = jnp.exp2(BITS - power)

    def code(value):
        return jnp.clip(jnp.round(value * scale), -TOP, TOP).astype(jnp.int32)

    biased = power.astype(jnp.int32) + BIAS
    row = lax.broadcasted_iota(jnp.int32, own.shape, 0) % 4
    part = jnp.where(row == 0, biased & 15, jnp.where(row == 1, biased >> 4, 0))
    mine = code(own)
    first = (code(real) << 12) | ((mine >> 8) & 4095)
    second = (code(imag) << 12) | ((mine & 255) << 4) | part
    return first, second


def unit_of(tile):
    part = tile & 15
    biased = part[4:5] + (part[5:6] << 4)
    return jnp.exp2((biased - (BIAS + BITS)).astype(jnp.float32))


def kernel(
    blocks_hbm, trial_ref, occupied, kpoint_map, partner, plus_ref, minus_ref,
    blocks, stage, work, masked, trials, outgoing, incoming,
    load_sem, block_send, block_recv, trial_send, trial_recv, term_send, term_recv,
):
    me, v = lax.axis_index("pb"), lax.axis_index("vert")
    zl, x, c = me // 8, (me // 2) % 4, me % 2
    zh, y = v // 4, v % 4
    z = zh * 8 + zl
    source_y = (x + zl) % 4
    mine = source_y == y
    trial_y = (x - z + 16) % 4
    trial_mine = mine & (trial_y == y)

    load = pltpu.make_async_copy(blocks_hbm, blocks, load_sem)
    load.start()

    barrier = pltpu.get_barrier_semaphore()

    def greet(pb, vert):
        pl.semaphore_signal(barrier, inc=1, device_id=(pb, vert), device_id_type=MESH)

    for d in range(1, 4):
        greet(me, zh * 4 + (y + d) % 4)

    def greet_terms(i, carry):
        for h in range(2):
            w = h * 4 + source_y

            @pl.when(jnp.logical_not((i == me) & (w == v)))
            def _():
                greet(i, w)

        return carry

    lax.fori_loop(0, 64, greet_terms, 0)

    def greet_trials(jp, carry):
        near = (z + (jp - z + 4 + 16) % 8 - 4 + 16) % 16
        w = (near // 8) * 4 + trial_y
        for cp in range(2):
            k = kpoint(jp, cp, y)

            @pl.when(jnp.logical_not((k == me) & (w == v)))
            def _():
                greet(k, w)

        return carry

    lax.fori_loop(0, 8, greet_trials, 0)

    live = lax.broadcasted_iota(jnp.int32, (32, 128), 0) < occupied[me]
    for part in range(2):
        value = trial_ref[part].astype(jnp.float32)
        masked[part] = jnp.where(live, value, 0.0).astype(jnp.bfloat16)

    away = pl.multiple_of((1 - zh) * 64, 64)

    def clear(jp, carry):
        for cp in range(2):
            for part in range(2):
                work[jp, cp, 1, part, pl.ds(away, 64), :] = jnp.zeros((64, 128), jnp.bfloat16)
        return carry

    lax.fori_loop(0, 8, clear, 0)
    load.wait()
    mirror_q = partner[me]

    def arrange(jp, carry):
        for to in range(4):
            for cp in range(2):
                k = kpoint(jp, cp, to)
                stage[to, jp, cp, 0, 0] = blocks[k, 0]
                stage[to, jp, cp, 0, 1] = -blocks[k, 1]
                stage[to, jp, cp, 1] = blocks[kpoint_map[mirror_q, k]]
        return carry

    lax.fori_loop(0, 8, arrange, 0)

    met = 147 - mine.astype(jnp.int32) - trial_mine.astype(jnp.int32)
    pl.semaphore_wait(barrier, met)

    def rows_from(jp, source):
        start = pl.multiple_of(zh * 64 + source * 16, 16)
        return work.at[jp, :, :, :, pl.ds(start, 16), :]

    def block_copy(i, d, source, target):
        jp = (zl + i) % 8
        return pltpu.make_async_remote_copy(
            src_ref=stage.at[target, jp],
            dst_ref=rows_from(jp, source),
            send_sem=block_send,
            recv_sem=block_recv.at[i, d],
            device_id=(me, zh * 4 + target),
            device_id_type=MESH,
        )

    def self_copy(i):
        jp = (zl + i) % 8
        return pltpu.make_async_copy(stage.at[y, jp], rows_from(jp, y), block_recv.at[i, 0])

    def trial_sends(i, carry):
        there = (z - ((i + 4) % 8 - 4) + 16) % 16
        x_to = (y + there) % 4
        w = (there // 8) * 4 + source_y
        slot = 2 * zl + c
        for cp in range(2):
            q = (there % 8) * 8 + x_to * 2 + cp
            own = (q == me) & (w == v)

            @pl.when(own)
            def _():
                pltpu.make_async_copy(masked, trials.at[slot], trial_recv.at[slot]).start()

            @pl.when(jnp.logical_not(own))
            def _():
                pltpu.make_async_remote_copy(
                    src_ref=masked,
                    dst_ref=trials.at[slot],
                    send_sem=trial_send,
                    recv_sem=trial_recv.at[slot],
                    device_id=(q, w),
                    device_id_type=MESH,
                ).start()

        return carry

    def block_sends(i, carry):
        self_copy(i).start()
        for d in range(1, 4):
            block_copy(i, d, y, (y + d) % 4).start()
        return carry

    block_sends(0, 0)
    lax.fori_loop(0, 8, trial_sends, 0)
    lax.fori_loop(1, 8, block_sends, 0)

    here = pl.multiple_of(zh * 64, 64)
    low = lax.broadcasted_iota(jnp.int32, (8, 128), 0) < 4

    def terms(i, carry):
        jp = (zl + i) % 8
        self_copy(i).wait()
        for d in range(1, 4):
            block_copy(i, d, (y - d + 4) % 4, y).wait_recv()
        for cp in range(2):
            slot = 2 * jp + cp
            pltpu.make_async_copy(masked, trials.at[slot], trial_recv.at[slot]).wait()
            real, imag = trials[slot, 0], trials[slot, 1]
            left = jnp.concatenate(
                [jnp.concatenate([real, imag], axis=1), jnp.concatenate([imag, -real], axis=1)], axis=0
            )
            mirror = jnp.dot(left, work[jp, cp, 1].reshape(256, 128), preferred_element_type=jnp.float32)
            right = jnp.concatenate(
                [work[jp, cp, 0, 0, pl.ds(here, 64), :], work[jp, cp, 0, 1, pl.ds(here, 64), :]], axis=1
            )
            own = lax.dot_general(
                left, right, (((1,), (1,)), ((), ())), preferred_element_type=jnp.float32
            )
            own = jnp.concatenate([own[:32], own[32:]], axis=1)
            first, second = encode(own, mirror[:32], mirror[32:])
            k = kpoint(jp, cp, y)
            for t in range(4):
                one, two = first[8 * t : 8 * t + 8], second[8 * t : 8 * t + 8]
                outgoing[slot, 2 * t] = jnp.where(low, one, pltpu.roll(two, 4, 0))
                outgoing[slot, 2 * t + 1] = jnp.where(low, pltpu.roll(one, 4, 0), two)
            for w in range(8):
                own_tile = (k == me) & (w == v)

                @pl.when(own_tile)
                def _():
                    pltpu.make_async_copy(outgoing.at[slot, w], incoming.at[zh, me], term_recv).start()

                @pl.when(jnp.logical_not(own_tile))
                def _():
                    pltpu.make_async_remote_copy(
                        src_ref=outgoing.at[slot, w],
                        dst_ref=incoming.at[zh, me],
                        send_sem=term_send,
                        recv_sem=term_recv,
                        device_id=(k, w),
                        device_id_type=MESH,
                    ).start()

        return carry

    lax.fori_loop(0, 8, terms, 0)

    pltpu.make_async_copy(incoming, incoming, term_recv).wait()

    lane = lax.broadcasted_iota(jnp.int32, (8, 128), 1) < 64
    stay = low == lane
    sign = jnp.where(low, 0.5, -0.5)

    def finish(q):
        far0, far1 = incoming[0, q], incoming[1, q]
        high = jnp.where(low, far0, pltpu.roll(far1, 4, 0)) & 4095
        rest = (jnp.where(low, pltpu.roll(far0, 4, 0), far1) >> 4) & 255
        code = ((high << 20) | (rest << 12)) >> 12
        own = code.astype(jnp.float32) * jnp.where(low, unit_of(far0), unit_of(far1))
        own = jnp.where(stay, own, pltpu.roll(pltpu.roll(own, 4, 0), 64, 1))
        p = partner[q]
        near0, near1 = incoming[0, p], incoming[1, p]
        mirror = (near0 >> 12).astype(jnp.float32) * unit_of(near0) + (near1 >> 12).astype(jnp.float32) * unit_of(near1)
        return (own + mirror) * 0.5, pltpu.roll(own - mirror, 4, 0) * sign

    def close(i, carry):
        results = [finish(2 * i), finish(2 * i + 1)]
        start = pl.multiple_of(i * 16, 16)
        plus_ref[pl.ds(start, 16), :] = jnp.concatenate([r[0] for r in results], axis=0).astype(jnp.bfloat16)
        minus_ref[pl.ds(start, 16), :] = jnp.concatenate([r[1] for r in results], axis=0).astype(jnp.bfloat16)
        return carry

    lax.fori_loop(0, 32, close, 0, unroll=2)

    pltpu.make_async_copy(stage.at[0:3], stage.at[0:3], block_send).wait()

    @pl.when(trial_mine)
    def _():
        pltpu.make_async_copy(trials.at[0:15], trials.at[0:15], trial_send).wait()

    @pl.when(jnp.logical_not(trial_mine))
    def _():
        pltpu.make_async_copy(trials, trials, trial_send).wait()

    @pl.when(mine)
    def _():
        pltpu.make_async_copy(outgoing.at[0:15], outgoing.at[0:15], term_send).wait()
        pltpu.make_async_copy(outgoing.at[0, 0:7], outgoing.at[0, 0:7], term_send).wait()

    @pl.when(jnp.logical_not(mine))
    def _():
        pltpu.make_async_copy(outgoing, outgoing, term_send).wait()


def local(cholesky, trial_rows, occupied, kpoint_map, partner):
    blocks = cholesky.reshape(64, 2, 16, 128)
    trial = trial_rows.reshape(2, 32, 128)
    vmem = pl.BlockSpec(memory_space=pltpu.VMEM)
    smem = pl.BlockSpec(memory_space=pltpu.SMEM)
    bf16, i32 = jnp.bfloat16, jnp.int32
    plus, minus = pl.pallas_call(
        kernel,
        out_shape=[jax.ShapeDtypeStruct((512, 128), bf16)] * 2,
        in_specs=[pl.BlockSpec(memory_space=pl.ANY), vmem, smem, smem, smem],
        out_specs=[vmem, vmem],
        scratch_shapes=[
            pltpu.VMEM((64, 2, 16, 128), bf16),
            pltpu.VMEM((4, 8, 2, 2, 2, 16, 128), bf16),
            pltpu.VMEM((8, 2, 2, 2, 128, 128), bf16),
            pltpu.VMEM((2, 32, 128), bf16),
            pltpu.VMEM((16, 2, 32, 128), bf16),
            pltpu.VMEM((16, 8, 8, 128), i32),
            pltpu.VMEM((2, 64, 8, 128), i32),
            pltpu.SemaphoreType.DMA,
            pltpu.SemaphoreType.DMA,
            pltpu.SemaphoreType.DMA((8, 4)),
            pltpu.SemaphoreType.DMA,
            pltpu.SemaphoreType.DMA((16,)),
            pltpu.SemaphoreType.DMA,
            pltpu.SemaphoreType.DMA,
        ],
        compiler_params=pltpu.CompilerParams(
            collective_id=0, has_side_effects=True, vmem_limit_bytes=32 * 2**20
        ),
    )(blocks, trial, occupied, kpoint_map, partner)
    shape = (1, 64, 1, 2, 4, 128)
    return plus.reshape(shape), minus.reshape(shape)


def solution(mesh):
    in_specs = (P("pb", None, None, None, "vert", None), P("pb", None, None, None), P(), P(), P())
    out_specs = (P("pb", None, None, None, "vert", None), P("pb", None, None, None, "vert", None))
    return jax.shard_map(local, mesh=mesh, in_specs=in_specs, out_specs=out_specs, check_vma=False)
```

time: 275 us -> 76.2 us (0.28); the launches traced: 270 us -> 75.7 us
  waiting for transfers between devices: 182 us -> 0 us
  Pallas kernels: 0 us -> 70.6 us
  starting transfers between devices: 43.2 us -> 0 us
  between operations: 16.3 us -> 0.66 us
  local copies, waits for them, and re-layouts: 18.5 us -> 4.48 us
  other arithmetic: 6.02 us -> 0 us
  matrix products: 3.15 us -> 0 us
    all_gather x1 -> x0, waiting for transfers between devices: 106 us -> none  [local(): gathered = lax.all_gather(trial_rows, 'pb', axis=0, tiled=True)]
    all_to_all x5 -> x0, waiting for transfers between devices: 75.7 us -> none  [the longest x1 17 us: local(): lax.all_to_all(mirror_out, 'pb', split_axis=0, concat_axis=0, tiled=True)]
    pallas_call x0 -> x1, Pallas kernels: none -> 70.6 us  [local(): pl.pallas_call(kernel, out_shape=[jax.ShapeDtypeStruct((512, 128), bf16)]...]
    all_to_all x5 -> x0, starting transfers between devices: 43.2 us -> none  [the longest x1 18.3 us: local(): lax.all_to_all(ready_blk, 'vert', split_axis=4, concat_axis=3, tiled=True)]
    unnamed x21 -> x12, local copies, waits for them, and re-layouts: 10.2 us -> 4.48 us
    dot_general x8 -> x0, matrix products: 3.15 us -> none  [product(): return jnp.einsum(pattern, left, right, preferred_element_type=jnp.float32)]
    gather x3 -> x0, local copies, waits for them, and re-layouts: 3.07 us -> none  [the longest x1 1.7 us: local(): ready_blk = jnp.take(own_blk, order_rows, axis=0)]
  transfers between devices with their start and end apart: 6 -> 0, of which waited for: 6 -> 0; matrix products, arithmetic and copies ran while one was open for 4% -> 0% of each run, Pallas kernels for 0% -> 0%
where the time goes in v1:
time: 76.2 us; the launch traced here: 75.7 us
  Pallas kernels  70.6 us (93%)
  local copies, waits for them, and re-layouts  4.48 us (6%)
    pallas_call x1, Pallas kernels, local(): pl.pallas_call(kernel, out_shape=[jax.ShapeDtypeStruct((512, 128), bf16)]...  70.6 us
    unnamed x12, local copies, waits for them, and re-layouts  4.48 us

profile of v1, /device:TPU:1, one launch (start us, length us, event | category | flops | bytes accessed | tf_op | source)
XLA Modules:
  0.0 75.7 jit_solution(13351615474979854387)
XLA Ops:
  0.6 0.0 copy-start.3
  0.6 0.0 copy-start.4
  0.7 0.6 copy-done.3
  1.3 0.0 copy-done.4
  1.3 0.0 copy-start
  1.3 1.0 %copy-done = bf16[1,64,1,2,16,128]{5,4,3,2,1,0:T(8,128)(2,1)S(1)} copy-done((bf16[1,64,1,2,16,128]{5,4,3,2,1,0:T(8,128)(2,1)S(1)}, bf16[1,64,1,2,16,128]{5,4,3,2,1,0:T(8,128)(2,1)}, u32[]{:S(2)}) %copy-start) | copy-done | bytes 524312
  2.3 0.0 copy-start.1
  2.3 0.8 copy-done.1
  3.1 0.0 copy-start.2
  3.1 0.7 copy-done.2
  3.8 70.6 %shard_map.68 = (bf16[512,128]{1,0:T(8,128)(2,1)S(1)}, bf16[512,128]{1,0:T(8,128)(2,1)S(1)}) custom-call(bf16[64,2,16,128]{3,2,1,0:T(8,128)(2,1)S(1)} %bitcast.8, bf16[2,32,128]{2,1,0:T(8,128)(2,1)S(1)} %bitcast.11, s32[64]{0:T(128)S(1)} %copy-done.3, s32[64,64]{1,0:T(8,128)S(1)} %copy-done.1, s32[64]{0:T(128)S(1)} %copy-done.4), custom_call_target="tpu_custom_call" | custom-call | tf_op jit(solution)/shard_map/pallas_call | solution.py:285
  74.4 0.7 copy.11
  75.1 0.7 copy.12
Async XLA Ops:
  0.6 0.7 copy-start.3
  0.6 0.7 copy-start.4
  1.3 1.0 %copy-start = (bf16[1,64,1,2,16,128]{5,4,3,2,1,0:T(8,128)(2,1)S(1)}, bf16[1,64,1,2,16,128]{5,4,3,2,1,0:T(8,128)(2,1)}, u32[]{:S(2)}) copy-start(bf16[1,64,1,2,16,128]{5,4,3,2,1,0:T(8,128)(2,1)} %param.5) | copy-start | bytes 1572868
  2.3 0.8 %copy-start.1 = (s32[64,64]{1,0:T(8,128)S(1)}, s32[64,64]{1,0:T(8,128)}, u32[]{:S(2)}) copy-start(s32[64,64]{1,0:T(8,128)} %kpoint_map.1) | copy-start | bytes 49156
  3.1 0.7 copy-start.2

commit v2 on v1

--- a/solution.py
+++ b/solution.py
@@ -42,8 +42,8 @@
 
 
 def kernel(
-    blocks_hbm, trial_ref, occupied, kpoint_map, partner, plus_ref, minus_ref,
-    blocks, stage, work, masked, trials, outgoing, incoming,
+    blocks_hbm, trial_hbm, occupied_hbm, map_hbm, partner_hbm, plus_ref, minus_ref,
+    blocks, trial_ref, occupied, kpoint_map, partner, stage, work, trials, outgoing, incoming,
     load_sem, block_send, block_recv, trial_send, trial_recv, term_send, term_recv,
 ):
     me, v = lax.axis_index("pb"), lax.axis_index("vert")
@@ -52,11 +52,12 @@
     z = zh * 8 + zl
     source_y = (x + zl) % 4
     mine = source_y == y
-    trial_y = (x - z + 16) % 4
-    trial_mine = mine & (trial_y == y)
-
-    load = pltpu.make_async_copy(blocks_hbm, blocks, load_sem)
-    load.start()
+    slot_me = 2 * zl + c
+    first_zl = (zl + (y - x - zl + 12) % 4) % 8
+    second_zl = (first_zl + 4) % 8
+
+    def nearest(there):
+        return (z + (there - z + 4 + 16) % 8 - 4 + 16) % 16
 
     barrier = pltpu.get_barrier_semaphore()
 
@@ -78,24 +79,25 @@
 
     lax.fori_loop(0, 64, greet_terms, 0)
 
-    def greet_trials(jp, carry):
-        near = (z + (jp - z + 4 + 16) % 8 - 4 + 16) % 16
-        w = (near // 8) * 4 + trial_y
-        for cp in range(2):
-            k = kpoint(jp, cp, y)
-
-            @pl.when(jnp.logical_not((k == me) & (w == v)))
-            def _():
-                greet(k, w)
-
-        return carry
-
-    lax.fori_loop(0, 8, greet_trials, 0)
-
-    live = lax.broadcasted_iota(jnp.int32, (32, 128), 0) < occupied[me]
-    for part in range(2):
-        value = trial_ref[part].astype(jnp.float32)
-        masked[part] = jnp.where(live, value, 0.0).astype(jnp.bfloat16)
+    for i in range(1, 8):
+        greet(zl * 8 + ((x + i // 2) % 4) * 2 + (c + i) % 2, v)
+
+    @pl.when(jnp.logical_not(mine))
+    def _():
+        near = nearest(first_zl)
+        greet(first_zl * 8 + x * 2 + c, (near // 8) * 4 + y)
+
+    near = nearest(second_zl)
+    greet(second_zl * 8 + x * 2 + c, (near // 8) * 4 + y)
+
+    loads = [
+        pltpu.make_async_copy(a, b, load_sem.at[n])
+        for n, (a, b) in enumerate(
+            [(blocks_hbm, blocks), (trial_hbm, trial_ref), (occupied_hbm, occupied), (map_hbm, kpoint_map), (partner_hbm, partner)]
+        )
+    ]
+    for load in loads:
+        load.start()
 
     away = pl.multiple_of((1 - zh) * 64, 64)
 
@@ -106,7 +108,16 @@
         return carry
 
     lax.fori_loop(0, 8, clear, 0)
-    load.wait()
+    for load in loads:
+        load.wait()
+
+    @pl.when(mine)
+    def _():
+        live = lax.broadcasted_iota(jnp.int32, (32, 128), 0) < occupied[me]
+        for part in range(2):
+            value = trial_ref[part].astype(jnp.float32)
+            trials[slot_me, part] = jnp.where(live, value, 0.0).astype(jnp.bfloat16)
+
     mirror_q = partner[me]
 
     def arrange(jp, carry):
@@ -120,8 +131,7 @@
 
     lax.fori_loop(0, 8, arrange, 0)
 
-    met = 147 - mine.astype(jnp.int32) - trial_mine.astype(jnp.int32)
-    pl.semaphore_wait(barrier, met)
+    pl.semaphore_wait(barrier, 138 + 6 * mine.astype(jnp.int32))
 
     def rows_from(jp, source):
         start = pl.multiple_of(zh * 64 + source * 16, 16)
@@ -142,31 +152,19 @@
         jp = (zl + i) % 8
         return pltpu.make_async_copy(stage.at[y, jp], rows_from(jp, y), block_recv.at[i, 0])
 
-    def trial_sends(i, carry):
-        there = (z - ((i + 4) % 8 - 4) + 16) % 16
-        x_to = (y + there) % 4
-        w = (there // 8) * 4 + source_y
-        slot = 2 * zl + c
-        for cp in range(2):
-            q = (there % 8) * 8 + x_to * 2 + cp
-            own = (q == me) & (w == v)
-
-            @pl.when(own)
-            def _():
-                pltpu.make_async_copy(masked, trials.at[slot], trial_recv.at[slot]).start()
-
-            @pl.when(jnp.logical_not(own))
-            def _():
-                pltpu.make_async_remote_copy(
-                    src_ref=masked,
-                    dst_ref=trials.at[slot],
-                    send_sem=trial_send,
-                    recv_sem=trial_recv.at[slot],
-                    device_id=(q, w),
-                    device_id_type=MESH,
-                ).start()
-
-        return carry
+    def trial_copy(slot, pb, vert):
+        return pltpu.make_async_remote_copy(
+            src_ref=trials.at[slot],
+            dst_ref=trials.at[slot],
+            send_sem=trial_send,
+            recv_sem=trial_recv.at[slot],
+            device_id=(pb, vert),
+            device_id_type=MESH,
+        )
+
+    def forward(there):
+        for i in range(1, 8):
+            trial_copy(2 * there + c, zl * 8 + ((x + i // 2) % 4) * 2 + (c + i) % 2, v).start()
 
     def block_sends(i, carry):
         self_copy(i).start()
@@ -174,21 +172,47 @@
             block_copy(i, d, y, (y + d) % 4).start()
         return carry
 
+    @pl.when(mine)
+    def _():
+        forward(zl)
+        for d in (1, -1, 2, -2, 3, -3, -4):
+            there = (z - d + 16) % 16
+            trial_copy(slot_me, (there % 8) * 8 + x * 2 + c, (there // 8) * 4 + y).start()
+
     block_sends(0, 0)
-    lax.fori_loop(0, 8, trial_sends, 0)
-    lax.fori_loop(1, 8, block_sends, 0)
+    block_sends(1, 0)
+
+    @pl.when(jnp.logical_not(mine))
+    def _():
+        trial_copy(2 * first_zl + c, me, v).wait_recv()
+        forward(first_zl)
+
 
     here = pl.multiple_of(zh * 64, 64)
     low = lax.broadcasted_iota(jnp.int32, (8, 128), 0) < 4
 
     def terms(i, carry):
         jp = (zl + i) % 8
+
+        @pl.when(i < 6)
+        def _():
+            block_sends(i + 2, 0)
+
+        @pl.when(i == 1)
+        def _():
+            trial_copy(2 * second_zl + c, me, v).wait_recv()
+            forward(second_zl)
+
         self_copy(i).wait()
         for d in range(1, 4):
             block_copy(i, d, (y - d + 4) % 4, y).wait_recv()
         for cp in range(2):
             slot = 2 * jp + cp
-            pltpu.make_async_copy(masked, trials.at[slot], trial_recv.at[slot]).wait()
+
+            @pl.when((cp != c) | ((jp != first_zl) & (jp != second_zl)))
+            def _():
+                trial_copy(slot, me, v).wait_recv()
+
             real, imag = trials[slot, 0], trials[slot, 1]
             left = jnp.concatenate(
                 [jnp.concatenate([real, imag], axis=1), jnp.concatenate([imag, -real], axis=1)], axis=0
@@ -258,13 +282,11 @@
 
     pltpu.make_async_copy(stage.at[0:3], stage.at[0:3], block_send).wait()
 
-    @pl.when(trial_mine)
-    def _():
-        pltpu.make_async_copy(trials.at[0:15], trials.at[0:15], trial_send).wait()
-
-    @pl.when(jnp.logical_not(trial_mine))
-    def _():
-        pltpu.make_async_copy(trials, trials, trial_send).wait()
+    pltpu.make_async_copy(trials.at[0:14], trials.at[0:14], trial_send).wait()
+
+    @pl.when(mine)
+    def _():
+        pltpu.make_async_copy(trials.at[0:7], trials.at[0:7], trial_send).wait()
 
     @pl.when(mine)
     def _():
@@ -280,22 +302,24 @@
     blocks = cholesky.reshape(64, 2, 16, 128)
     trial = trial_rows.reshape(2, 32, 128)
     vmem = pl.BlockSpec(memory_space=pltpu.VMEM)
-    smem = pl.BlockSpec(memory_space=pltpu.SMEM)
     bf16, i32 = jnp.bfloat16, jnp.int32
     plus, minus = pl.pallas_call(
         kernel,
         out_shape=[jax.ShapeDtypeStruct((512, 128), bf16)] * 2,
-        in_specs=[pl.BlockSpec(memory_space=pl.ANY), vmem, smem, smem, smem],
+        in_specs=[pl.BlockSpec(memory_space=pl.ANY)] * 5,
         out_specs=[vmem, vmem],
         scratch_shapes=[
             pltpu.VMEM((64, 2, 16, 128), bf16),
+            pltpu.VMEM((2, 32, 128), bf16),
+            pltpu.SMEM((64,), i32),
+            pltpu.SMEM((64, 64), i32),
+            pltpu.SMEM((64,), i32),
             pltpu.VMEM((4, 8, 2, 2, 2, 16, 128), bf16),
             pltpu.VMEM((8, 2, 2, 2, 128, 128), bf16),
-            pltpu.VMEM((2, 32, 128), bf16),
             pltpu.VMEM((16, 2, 32, 128), bf16),
             pltpu.VMEM((16, 8, 8, 128), i32),
             pltpu.VMEM((2, 64, 8, 128), i32),
-            pltpu.SemaphoreType.DMA,
+            pltpu.SemaphoreType.DMA((5,)),
             pltpu.SemaphoreType.DMA,
             pltpu.SemaphoreType.DMA((8, 4)),
             pltpu.SemaphoreType.DMA,
@@ -304,7 +328,7 @@
             pltpu.SemaphoreType.DMA,
         ],
         compiler_params=pltpu.CompilerParams(
-            collective_id=0, has_side_effects=True, vmem_limit_bytes=32 * 2**20
+            collective_id=0, has_side_effects=True, vmem_limit_bytes=60 * 2**20
         ),
     )(blocks, trial, occupied, kpoint_map, partner)
     shape = (1, 64, 1, 2, 4, 128)

time: 76.2 us -> 66 us (0.87)
  Pallas kernels: 70.6 us -> 62.8 us
  local copies, waits for them, and re-layouts: 4.48 us -> 2.3 us
    pallas_call x1, Pallas kernels: 70.6 us -> 62.8 us  [local(): pl.pallas_call(kernel, out_shape=[jax.ShapeDtypeStruct((512, 128), bf16)]...]
    unnamed x12 -> x4, local copies, waits for them, and re-layouts: 4.48 us -> 2.3 us
where the time goes in v2:
time: 66 us; the launch traced here: 65.8 us
  Pallas kernels  62.8 us (95%)
  local copies, waits for them, and re-layouts  2.3 us (3%)
    pallas_call x1, Pallas kernels, local(): pl.pallas_call(kernel, out_shape=[jax.ShapeDtypeStruct((512, 128), bf16)]...  62.8 us
    unnamed x4, local copies, waits for them, and re-layouts  2.3 us

profile of v2, /device:TPU:1, one launch (start us, length us, event | category | flops | bytes accessed | tf_op | source)
XLA Modules:
  0.0 65.8 jit_solution(175624171324722151)
XLA Ops:
  0.6 62.8 %shard_map.68 = (bf16[512,128]{1,0:T(8,128)(2,1)}, bf16[512,128]{1,0:T(8,128)(2,1)}) custom-call(bf16[64,2,16,128]{3,2,1,0:T(8,128)(2,1)} %bitcast.8, bf16[2,32,128]{2,1,0:T(8,128)(2,1)} %bitcast.11, s32[64]{0:T(128)} %occupied_hbm.1, s32[64,64]{1,0:T(8,128)} %map_hbm.1, s32[64]{0:T(128)} %partner_hbm.1), custom_call_target="tpu_custom_call" | custom-call | tf_op jit(solution)/shard_map/pallas_call | solution.py:306
  63.5 0.0 copy-start
  63.5 1.6 %copy.11 = bf16[1,64,1,2,4,128]{5,4,3,2,1,0:T(4,128)(2,1)} copy(bf16[1,64,1,2,4,128]{5,4,3,2,1,0:T(4,128)(2,1)} %bitcast.10) | data formatting | bytes 262144
  65.1 0.0 copy-done
  65.1 0.7 copy.12
Async XLA Ops:
  63.5 1.7 %copy-start = (bf16[512,128]{1,0:T(8,128)(2,1)S(1)}, bf16[512,128]{1,0:T(8,128)(2,1)}, u32[]{:S(2)}) copy-start(bf16[512,128]{1,0:T(8,128)(2,1)} %get-tuple-element.5) | copy-start | bytes 393220

commit v3 on v2

--- a/solution.py
+++ b/solution.py
@@ -8,7 +8,7 @@
 from jax.sharding import PartitionSpec as P
 
 MESH = pl.DeviceIdType.MESH
-BITS = 19
+BITS = 17
 TOP = 2**BITS - 1
 BIAS = 128
 
@@ -22,23 +22,30 @@
     peak = jnp.max(peak, axis=0, keepdims=True)
     power = jnp.floor(jnp.log2(jnp.maximum(peak, 2.0**-100))) + 1.0
     scale = jnp.exp2(BITS - power)
-
-    def code(value):
-        return jnp.clip(jnp.round(value * scale), -TOP, TOP).astype(jnp.int32)
-
-    biased = power.astype(jnp.int32) + BIAS
-    row = lax.broadcasted_iota(jnp.int32, own.shape, 0) % 4
-    part = jnp.where(row == 0, biased & 15, jnp.where(row == 1, biased >> 4, 0))
-    mine = code(own)
-    first = (code(real) << 12) | ((mine >> 8) & 4095)
-    second = (code(imag) << 12) | ((mine & 255) << 4) | part
-    return first, second
-
-
-def unit_of(tile):
-    part = tile & 15
-    biased = part[4:5] + (part[5:6] << 4)
-    return jnp.exp2((biased - (BIAS + BITS)).astype(jnp.float32))
+    biased = (power.astype(jnp.int32) + BIAS) << 24
+    row = lax.broadcasted_iota(jnp.int32, (8, 128), 0)
+    low = row < 4
+    place = (row % 4) * 6
+
+    def code(value, t):
+        return jnp.clip(jnp.round(value[8 * t : 8 * t + 8] * scale), -TOP, TOP).astype(jnp.int32)
+
+    messages = []
+    for t in range(4):
+        a, b, c = code(real, t), code(imag, t), code(own, t)
+        mirror = ((a >> 2) << 16) | ((b >> 2) & 65535)
+        pairs = ((c >> 2) << 16) | pltpu.roll((c >> 2) & 65535, 6, 0)
+        small = (((a & 3) << 4) | ((b & 3) << 2) | (c & 3)) << place
+        small = small + pltpu.roll(small, 7, 0)
+        small = (small + pltpu.roll(small, 6, 0)) | biased
+        rest = jnp.where(row % 4 < 2, pairs, pltpu.roll(small, 2, 0))
+        messages.append(jnp.where(low, mirror, pltpu.roll(rest, 4, 0)))
+        messages.append(jnp.where(low, pltpu.roll(mirror, 4, 0), rest))
+    return messages
+
+
+def unit_of(word):
+    return jnp.exp2((((word >> 24) & 255) - (BIAS + BITS)).astype(jnp.float32))
 
 
 def kernel(
@@ -172,6 +179,8 @@
             block_copy(i, d, y, (y + d) % 4).start()
         return carry
 
+    block_sends(0, 0)
+
     @pl.when(mine)
     def _():
         forward(zl)
@@ -179,7 +188,6 @@
             there = (z - d + 16) % 16
             trial_copy(slot_me, (there % 8) * 8 + x * 2 + c, (there // 8) * 4 + y).start()
 
-    block_sends(0, 0)
     block_sends(1, 0)
 
     @pl.when(jnp.logical_not(mine))
@@ -225,12 +233,10 @@
                 left, right, (((1,), (1,)), ((), ())), preferred_element_type=jnp.float32
             )
             own = jnp.concatenate([own[:32], own[32:]], axis=1)
-            first, second = encode(own, mirror[:32], mirror[32:])
+            messages = encode(own, mirror[:32], mirror[32:])
             k = kpoint(jp, cp, y)
-            for t in range(4):
-                one, two = first[8 * t : 8 * t + 8], second[8 * t : 8 * t + 8]
-                outgoing[slot, 2 * t] = jnp.where(low, one, pltpu.roll(two, 4, 0))
-                outgoing[slot, 2 * t + 1] = jnp.where(low, pltpu.roll(one, 4, 0), two)
+            for w in range(8):
+                outgoing[slot, w] = messages[w][:7]
             for w in range(8):
                 own_tile = (k == me) & (w == v)
 
@@ -259,16 +265,31 @@
     stay = low == lane
     sign = jnp.where(low, 0.5, -0.5)
 
+    row = lax.broadcasted_iota(jnp.int32, (8, 128), 0)
+    own_place = (row % 4) * 6
+    mirror_place = own_place + jnp.where(low, 4, 2)
+
+    def own_of(q):
+        parts = []
+        for h in range(2):
+            pairs = incoming[h, q, pl.ds(4, 2)]
+            parts += [pairs >> 16, (pairs << 16) >> 16]
+        first, second = incoming[0, q, pl.ds(6, 1)], incoming[1, q, pl.ds(6, 1)]
+        small = (jnp.where(low, first, second) >> own_place) & 3
+        code = (jnp.concatenate(parts, axis=0) << 2) | small
+        own = code.astype(jnp.float32) * jnp.where(low, unit_of(first), unit_of(second))
+        return jnp.where(stay, own, pltpu.roll(pltpu.roll(own, 4, 0), 64, 1))
+
+    def mirror_of(p, h):
+        words, last = incoming[h, p, pl.ds(0, 4)], incoming[h, p, pl.ds(6, 1)]
+        code = jnp.concatenate([words >> 16, (words << 16) >> 16], axis=0)
+        code = (code << 2) | ((last >> mirror_place) & 3)
+        return code.astype(jnp.float32) * unit_of(last)
+
     def finish(q):
-        far0, far1 = incoming[0, q], incoming[1, q]
-        high = jnp.where(low, far0, pltpu.roll(far1, 4, 0)) & 4095
-        rest = (jnp.where(low, pltpu.roll(far0, 4, 0), far1) >> 4) & 255
-        code = ((high << 20) | (rest << 12)) >> 12
-        own = code.astype(jnp.float32) * jnp.where(low, unit_of(far0), unit_of(far1))
-        own = jnp.where(stay, own, pltpu.roll(pltpu.roll(own, 4, 0), 64, 1))
+        own = own_of(q)
         p = partner[q]
-        near0, near1 = incoming[0, p], incoming[1, p]
-        mirror = (near0 >> 12).astype(jnp.float32) * unit_of(near0) + (near1 >> 12).astype(jnp.float32) * unit_of(near1)
+        mirror = mirror_of(p, 0) + mirror_of(p, 1)
         return (own + mirror) * 0.5, pltpu.roll(own - mirror, 4, 0) * sign
 
     def close(i, carry):
@@ -317,8 +338,8 @@
             pltpu.VMEM((4, 8, 2, 2, 2, 16, 128), bf16),
             pltpu.VMEM((8, 2, 2, 2, 128, 128), bf16),
             pltpu.VMEM((16, 2, 32, 128), bf16),
-            pltpu.VMEM((16, 8, 8, 128), i32),
-            pltpu.VMEM((2, 64, 8, 128), i32),
+            pltpu.VMEM((16, 8, 7, 128), i32),
+            pltpu.VMEM((2, 64, 7, 128), i32),
             pltpu.SemaphoreType.DMA((5,)),
             pltpu.SemaphoreType.DMA,
             pltpu.SemaphoreType.DMA((8, 4)),

time: 66 us -> 62.8 us (0.952)
  Pallas kernels: 62.8 us -> 59.1 us
    pallas_call x1, Pallas kernels: 62.8 us -> 59.1 us  [local(): pl.pallas_call(kernel, out_shape=[jax.ShapeDtypeStruct((512, 128), bf16)]...]
where the time goes in v3:
time: 62.8 us; the launch traced here: 62 us
  Pallas kernels  59.1 us (94%)
  local copies, waits for them, and re-layouts  2.3 us (4%)
  between operations  0.65 us (1%)
    pallas_call x1, Pallas kernels, local(): pl.pallas_call(kernel, out_shape=[jax.ShapeDtypeStruct((512, 128), bf16)]...  59.1 us
    unnamed x4, local copies, waits for them, and re-layouts  2.3 us

profile of v3, /device:TPU:1, one launch (start us, length us, event | category | flops | bytes accessed | tf_op | source)
XLA Modules:
  0.0 62.0 jit_solution(2483168932482436689)
XLA Ops:
  0.6 59.1 %shard_map.68 = (bf16[512,128]{1,0:T(8,128)(2,1)}, bf16[512,128]{1,0:T(8,128)(2,1)}) custom-call(bf16[64,2,16,128]{3,2,1,0:T(8,128)(2,1)} %bitcast.8, bf16[2,32,128]{2,1,0:T(8,128)(2,1)} %bitcast.11, s32[64]{0:T(128)} %occupied_hbm.1, s32[64,64]{1,0:T(8,128)} %map_hbm.1, s32[64]{0:T(128)} %partner_hbm.1), custom_call_target="tpu_custom_call" | custom-call | tf_op jit(solution)/shard_map/pallas_call | solution.py:327
  59.7 0.0 copy-start
  59.7 1.6 %copy.11 = bf16[1,64,1,2,4,128]{5,4,3,2,1,0:T(4,128)(2,1)} copy(bf16[1,64,1,2,4,128]{5,4,3,2,1,0:T(4,128)(2,1)} %bitcast.10) | data formatting | bytes 262144
  61.3 0.0 copy-done
  61.3 0.7 %copy.12 = bf16[1,64,1,2,4,128]{5,4,3,2,1,0:T(4,128)(2,1)} copy(bf16[1,64,1,2,4,128]{5,4,3,2,1,0:T(4,128)(2,1)S(1)} %bitcast.9) | data formatting | bytes 262144
Async XLA Ops:
  59.7 1.7 %copy-start = (bf16[512,128]{1,0:T(8,128)(2,1)S(1)}, bf16[512,128]{1,0:T(8,128)(2,1)}, u32[]{:S(2)}) copy-start(bf16[512,128]{1,0:T(8,128)(2,1)} %get-tuple-element.5) | copy-start | bytes 393220

commit v4 on v3

--- a/solution.py
+++ b/solution.py
@@ -13,8 +13,8 @@
 BIAS = 128
 
 
-def kpoint(jp, cp, y):
-    return jp * 8 + ((y - jp + 8) % 4) * 2 + cp
+def kpoint(jp, cp, y, zl):
+    return jp * 8 + ((y - jp + zl + 8) % 4) * 2 + cp
 
 
 def encode(own, real, imag):
@@ -50,17 +50,16 @@
 
 def kernel(
     blocks_hbm, trial_hbm, occupied_hbm, map_hbm, partner_hbm, plus_ref, minus_ref,
-    blocks, trial_ref, occupied, kpoint_map, partner, stage, work, trials, outgoing, incoming,
+    blocks, trial_ref, masked, occupied, kpoint_map, partner, stage, work, trials, outgoing, incoming,
     load_sem, block_send, block_recv, trial_send, trial_recv, term_send, term_recv,
 ):
     me, v = lax.axis_index("pb"), lax.axis_index("vert")
     zl, x, c = me // 8, (me // 2) % 4, me % 2
     zh, y = v // 4, v % 4
     z = zh * 8 + zl
-    source_y = (x + zl) % 4
-    mine = source_y == y
+    mine = x == y
     slot_me = 2 * zl + c
-    first_zl = (zl + (y - x - zl + 12) % 4) % 8
+    first_zl = (zl + (y - x + 4) % 4) % 8
     second_zl = (first_zl + 4) % 8
 
     def nearest(there):
@@ -76,7 +75,7 @@
 
     def greet_terms(i, carry):
         for h in range(2):
-            w = h * 4 + source_y
+            w = h * 4 + (x + zl - i // 8 + 8) % 4
 
             @pl.when(jnp.logical_not((i == me) & (w == v)))
             def _():
@@ -118,19 +117,21 @@
     for load in loads:
         load.wait()
 
+    live = lax.broadcasted_iota(jnp.int32, (32, 128), 0) < occupied[me]
+    for part in range(2):
+        value = trial_ref[part].astype(jnp.float32)
+        masked[part] = jnp.where(live, value, 0.0).astype(jnp.bfloat16)
+
     @pl.when(mine)
     def _():
-        live = lax.broadcasted_iota(jnp.int32, (32, 128), 0) < occupied[me]
-        for part in range(2):
-            value = trial_ref[part].astype(jnp.float32)
-            trials[slot_me, part] = jnp.where(live, value, 0.0).astype(jnp.bfloat16)
+        trials[slot_me] = masked[...]
 
     mirror_q = partner[me]
 
     def arrange(jp, carry):
         for to in range(4):
             for cp in range(2):
-                k = kpoint(jp, cp, to)
+                k = kpoint(jp, cp, to, zl)
                 stage[to, jp, cp, 0, 0] = blocks[k, 0]
                 stage[to, jp, cp, 0, 1] = -blocks[k, 1]
                 stage[to, jp, cp, 1] = blocks[kpoint_map[mirror_q, k]]
@@ -138,7 +139,7 @@
 
     lax.fori_loop(0, 8, arrange, 0)
 
-    pl.semaphore_wait(barrier, 138 + 6 * mine.astype(jnp.int32))
+    pl.semaphore_wait(barrier, 140 - 2 * mine.astype(jnp.int32))
 
     def rows_from(jp, source):
         start = pl.multiple_of(zh * 64 + source * 16, 16)
@@ -159,9 +160,9 @@
         jp = (zl + i) % 8
         return pltpu.make_async_copy(stage.at[y, jp], rows_from(jp, y), block_recv.at[i, 0])
 
-    def trial_copy(slot, pb, vert):
+    def trial_copy(slot, pb, vert, source=None):
         return pltpu.make_async_remote_copy(
-            src_ref=trials.at[slot],
+            src_ref=trials.at[slot] if source is None else source,
             dst_ref=trials.at[slot],
             send_sem=trial_send,
             recv_sem=trial_recv.at[slot],
@@ -181,13 +182,21 @@
 
     block_sends(0, 0)
 
+    def trial_along(d):
+        there = (z - d + 16) % 16
+        trial_copy(slot_me, (there % 8) * 8 + x * 2 + c, (there // 8) * 4 + y, masked).start()
+
+    offset = (y - x + 4) % 4
+
     @pl.when(mine)
     def _():
         forward(zl)
-        for d in (1, -1, 2, -2, 3, -3, -4):
-            there = (z - d + 16) % 16
-            trial_copy(slot_me, (there % 8) * 8 + x * 2 + c, (there // 8) * 4 + y).start()
-
+
+    @pl.when(jnp.logical_not(mine))
+    def _():
+        trial_along(offset)
+
+    trial_along(offset - 4)
     block_sends(1, 0)
 
     @pl.when(jnp.logical_not(mine))
@@ -234,7 +243,7 @@
             )
             own = jnp.concatenate([own[:32], own[32:]], axis=1)
             messages = encode(own, mirror[:32], mirror[32:])
-            k = kpoint(jp, cp, y)
+            k = kpoint(jp, cp, y, zl)
             for w in range(8):
                 outgoing[slot, w] = messages[w][:7]
             for w in range(8):
@@ -303,11 +312,11 @@
 
     pltpu.make_async_copy(stage.at[0:3], stage.at[0:3], block_send).wait()
 
-    pltpu.make_async_copy(trials.at[0:14], trials.at[0:14], trial_send).wait()
-
-    @pl.when(mine)
-    def _():
-        pltpu.make_async_copy(trials.at[0:7], trials.at[0:7], trial_send).wait()
+    pltpu.make_async_copy(trials.at[0:15], trials.at[0:15], trial_send).wait()
+
+    @pl.when(jnp.logical_not(mine))
+    def _():
+        pltpu.make_async_copy(trials.at[0], trials.at[0], trial_send).wait()
 
     @pl.when(mine)
     def _():
@@ -331,6 +340,7 @@
         out_specs=[vmem, vmem],
         scratch_shapes=[
             pltpu.VMEM((64, 2, 16, 128), bf16),
+            pltpu.VMEM((2, 32, 128), bf16),
             pltpu.VMEM((2, 32, 128), bf16),
             pltpu.SMEM((64,), i32),
             pltpu.SMEM((64, 64), i32),

time: 62.8 us -> 55.8 us (0.89)
  Pallas kernels: 59.1 us -> 52.5 us
    pallas_call x1, Pallas kernels: 59.1 us -> 52.5 us  [local(): pl.pallas_call(kernel, out_shape=[jax.ShapeDtypeStruct((512, 128), bf16)]...]
where the time goes in v4:
time: 55.8 us; the launch traced here: 55.5 us
  Pallas kernels  52.5 us (94%)
  local copies, waits for them, and re-layouts  2.3 us (4%)
  between operations  0.65 us (1%)
    pallas_call x1, Pallas kernels, local(): pl.pallas_call(kernel, out_shape=[jax.ShapeDtypeStruct((512, 128), bf16)]...  52.5 us
    unnamed x4, local copies, waits for them, and re-layouts  2.3 us

profile of v4, /device:TPU:1, one launch (start us, length us, event | category | flops | bytes accessed | tf_op | source)
XLA Modules:
  0.0 55.5 jit_solution(15010480168736610652)
XLA Ops:
  0.6 52.5 %shard_map.68 = (bf16[512,128]{1,0:T(8,128)(2,1)}, bf16[512,128]{1,0:T(8,128)(2,1)}) custom-call(bf16[64,2,16,128]{3,2,1,0:T(8,128)(2,1)} %bitcast.8, bf16[2,32,128]{2,1,0:T(8,128)(2,1)} %bitcast.11, s32[64]{0:T(128)} %occupied_hbm.1, s32[64,64]{1,0:T(8,128)} %map_hbm.1, s32[64]{0:T(128)} %partner_hbm.1), custom_call_target="tpu_custom_call" | custom-call | tf_op jit(solution)/shard_map/pallas_call | solution.py:336
  53.2 0.0 copy-start
  53.2 1.6 %copy.11 = bf16[1,64,1,2,4,128]{5,4,3,2,1,0:T(4,128)(2,1)} copy(bf16[1,64,1,2,4,128]{5,4,3,2,1,0:T(4,128)(2,1)} %bitcast.10) | data formatting | bytes 262144
  54.8 0.0 copy-done
  54.8 0.7 %copy.12 = bf16[1,64,1,2,4,128]{5,4,3,2,1,0:T(4,128)(2,1)} copy(bf16[1,64,1,2,4,128]{5,4,3,2,1,0:T(4,128)(2,1)S(1)} %bitcast.9) | data formatting | bytes 262144
Async XLA Ops:
  53.2 1.7 %copy-start = (bf16[512,128]{1,0:T(8,128)(2,1)S(1)}, bf16[512,128]{1,0:T(8,128)(2,1)}, u32[]{:S(2)}) copy-start(bf16[512,128]{1,0:T(8,128)(2,1)} %get-tuple-element.5) | copy-start | bytes 393220

commit v5 on v4

--- a/solution.py
+++ b/solution.py
@@ -50,8 +50,8 @@
 
 def kernel(
     blocks_hbm, trial_hbm, occupied_hbm, map_hbm, partner_hbm, plus_ref, minus_ref,
-    blocks, trial_ref, masked, occupied, kpoint_map, partner, stage, work, trials, outgoing, incoming,
-    load_sem, block_send, block_recv, trial_send, trial_recv, term_send, term_recv,
+    blocks, trial_ref, masked, occupied, kpoint_map, partner, stage, work, trials, outgoing, incoming, own_terms, mirror_terms,
+    plane_in, load_sem, block_send, block_recv, trial_send, trial_recv, term_send, term_recv,
 ):
     me, v = lax.axis_index("pb"), lax.axis_index("vert")
     zl, x, c = me // 8, (me // 2) % 4, me % 2
@@ -62,40 +62,6 @@
     first_zl = (zl + (y - x + 4) % 4) % 8
     second_zl = (first_zl + 4) % 8
 
-    def nearest(there):
-        return (z + (there - z + 4 + 16) % 8 - 4 + 16) % 16
-
-    barrier = pltpu.get_barrier_semaphore()
-
-    def greet(pb, vert):
-        pl.semaphore_signal(barrier, inc=1, device_id=(pb, vert), device_id_type=MESH)
-
-    for d in range(1, 4):
-        greet(me, zh * 4 + (y + d) % 4)
-
-    def greet_terms(i, carry):
-        for h in range(2):
-            w = h * 4 + (x + zl - i // 8 + 8) % 4
-
-            @pl.when(jnp.logical_not((i == me) & (w == v)))
-            def _():
-                greet(i, w)
-
-        return carry
-
-    lax.fori_loop(0, 64, greet_terms, 0)
-
-    for i in range(1, 8):
-        greet(zl * 8 + ((x + i // 2) % 4) * 2 + (c + i) % 2, v)
-
-    @pl.when(jnp.logical_not(mine))
-    def _():
-        near = nearest(first_zl)
-        greet(first_zl * 8 + x * 2 + c, (near // 8) * 4 + y)
-
-    near = nearest(second_zl)
-    greet(second_zl * 8 + x * 2 + c, (near // 8) * 4 + y)
-
     loads = [
         pltpu.make_async_copy(a, b, load_sem.at[n])
         for n, (a, b) in enumerate(
@@ -105,6 +71,23 @@
     for load in loads:
         load.start()
 
+    barrier = pltpu.get_barrier_semaphore()
+
+    def greet(pb, vert):
+        pl.semaphore_signal(barrier, inc=1, device_id=(pb, vert), device_id_type=MESH)
+
+    def greet_ring(i, carry):
+        there = (z + i) % 16
+        greet((there % 8) * 8 + x * 2 + c, (there // 8) * 4 + y)
+        return carry
+
+    def greet_plane(i, carry):
+        greet(zl * 8 + ((x + i // 8) % 4) * 2 + (c + i) % 2, zh * 4 + (y + i // 2) % 4)
+        return carry
+
+    lax.fori_loop(1, 16, greet_ring, 0, unroll=True)
+    lax.fori_loop(1, 32, greet_plane, 0, unroll=True)
+
     away = pl.multiple_of((1 - zh) * 64, 64)
 
     def clear(jp, carry):
@@ -139,7 +122,16 @@
 
     lax.fori_loop(0, 8, arrange, 0)
 
-    pl.semaphore_wait(barrier, 140 - 2 * mine.astype(jnp.int32))
+    pl.semaphore_wait(barrier, 46)
+
+    def tell_ring(i, carry):
+        there = (z + i) % 16
+        pl.semaphore_signal(
+            plane_in, inc=1, device_id=((there % 8) * 8 + x * 2 + c, (there // 8) * 4 + y), device_id_type=MESH
+        )
+        return carry
+
+    lax.fori_loop(1, 16, tell_ring, 0, unroll=True)
 
     def rows_from(jp, source):
         start = pl.multiple_of(zh * 64 + source * 16, 16)
@@ -197,7 +189,7 @@
         trial_along(offset)
 
     trial_along(offset - 4)
-    block_sends(1, 0)
+    lax.fori_loop(1, 8, block_sends, 0, unroll=True)
 
     @pl.when(jnp.logical_not(mine))
     def _():
@@ -205,20 +197,15 @@
         forward(first_zl)
 
 
+    trial_copy(2 * second_zl + c, me, v).wait_recv()
+    forward(second_zl)
+
     here = pl.multiple_of(zh * 64, 64)
     low = lax.broadcasted_iota(jnp.int32, (8, 128), 0) < 4
 
     def terms(i, carry):
         jp = (zl + i) % 8
 
-        @pl.when(i < 6)
-        def _():
-            block_sends(i + 2, 0)
-
-        @pl.when(i == 1)
-        def _():
-            trial_copy(2 * second_zl + c, me, v).wait_recv()
-            forward(second_zl)
 
         self_copy(i).wait()
         for d in range(1, 4):
@@ -246,12 +233,18 @@
             k = kpoint(jp, cp, y, zl)
             for w in range(8):
                 outgoing[slot, w] = messages[w][:7]
+            if cp == 0:
+
+                @pl.when(i == 0)
+                def _():
+                    pl.semaphore_wait(plane_in, 15)
+
             for w in range(8):
                 own_tile = (k == me) & (w == v)
 
                 @pl.when(own_tile)
                 def _():
-                    pltpu.make_async_copy(outgoing.at[slot, w], incoming.at[zh, me], term_recv).start()
+                    pltpu.make_async_copy(outgoing.at[slot, w], incoming.at[zh, me], term_recv.at[zl]).start()
 
                 @pl.when(jnp.logical_not(own_tile))
                 def _():
@@ -259,7 +252,7 @@
                         src_ref=outgoing.at[slot, w],
                         dst_ref=incoming.at[zh, me],
                         send_sem=term_send,
-                        recv_sem=term_recv,
+                        recv_sem=term_recv.at[zl],
                         device_id=(k, w),
                         device_id_type=MESH,
                     ).start()
@@ -267,8 +260,6 @@
         return carry
 
     lax.fori_loop(0, 8, terms, 0)
-
-    pltpu.make_async_copy(incoming, incoming, term_recv).wait()
 
     lane = lax.broadcasted_iota(jnp.int32, (8, 128), 1) < 64
     stay = low == lane
@@ -295,10 +286,23 @@
         code = (code << 2) | ((last >> mirror_place) & 3)
         return code.astype(jnp.float32) * unit_of(last)
 
+    def decode(o, carry):
+        start = pl.multiple_of((zl - o + 8) % 8 * 8, 8)
+        part = incoming.at[:, pl.ds(start, 8)]
+        pltpu.make_async_copy(part, part, term_recv.at[(zl - o + 8) % 8]).wait()
+
+        def one(n, carry):
+            q = start + n
+            own_terms[q] = own_of(q)
+            mirror_terms[q] = mirror_of(q, 0) + mirror_of(q, 1)
+            return carry
+
+        return lax.fori_loop(0, 8, one, carry, unroll=4)
+
+    lax.fori_loop(0, 8, decode, 0)
+
     def finish(q):
-        own = own_of(q)
-        p = partner[q]
-        mirror = mirror_of(p, 0) + mirror_of(p, 1)
+        own, mirror = own_terms[q], mirror_terms[partner[q]]
         return (own + mirror) * 0.5, pltpu.roll(own - mirror, 4, 0) * sign
 
     def close(i, carry):
@@ -308,7 +312,7 @@
         minus_ref[pl.ds(start, 16), :] = jnp.concatenate([r[1] for r in results], axis=0).astype(jnp.bfloat16)
         return carry
 
-    lax.fori_loop(0, 32, close, 0, unroll=2)
+    lax.fori_loop(0, 32, close, 0, unroll=4)
 
     pltpu.make_async_copy(stage.at[0:3], stage.at[0:3], block_send).wait()
 
@@ -350,18 +354,21 @@
             pltpu.VMEM((16, 2, 32, 128), bf16),
             pltpu.VMEM((16, 8, 7, 128), i32),
             pltpu.VMEM((2, 64, 7, 128), i32),
+            pltpu.VMEM((64, 8, 128), jnp.float32),
+            pltpu.VMEM((64, 8, 128), jnp.float32),
+            pltpu.SemaphoreType.REGULAR,
             pltpu.SemaphoreType.DMA((5,)),
             pltpu.SemaphoreType.DMA,
             pltpu.SemaphoreType.DMA((8, 4)),
             pltpu.SemaphoreType.DMA,
             pltpu.SemaphoreType.DMA((16,)),
             pltpu.SemaphoreType.DMA,
-            pltpu.SemaphoreType.DMA,
+            pltpu.SemaphoreType.DMA((8,)),
         ],
         compiler_params=pltpu.CompilerParams(
-            collective_id=0, has_side_effects=True, vmem_limit_bytes=60 * 2**20
+            collective_id=0, has_side_effects=True, vmem_limit_bytes=32 * 2**20
         ),
-    )(blocks, trial, occupied, kpoint_map, partner)
+    )(*[pltpu.with_memory_space_constraint(a, pltpu.HBM) for a in (blocks, trial, occupied, kpoint_map, partner)])
     shape = (1, 64, 1, 2, 4, 128)
     return plus.reshape(shape), minus.reshape(shape)
 

time: 55.8 us -> 52.2 us (0.935)
  Pallas kernels: 52.5 us -> 50.1 us
  local copies, waits for them, and re-layouts: 2.3 us -> 1.31 us
    pallas_call x1, Pallas kernels: 52.5 us -> 50.1 us  [local(): pl.pallas_call(kernel, out_shape=[jax.ShapeDtypeStruct((512, 128), bf16)]...]
    unnamed x4 -> x2, local copies, waits for them, and re-layouts: 2.3 us -> 1.31 us
where the time goes in v5:
time: 52.2 us; the launch traced here: 52.1 us
  Pallas kernels  50.1 us (96%)
  local copies, waits for them, and re-layouts  1.31 us (3%)
  between operations  0.64 us (1%)
    pallas_call x1, Pallas kernels, local(): pl.pallas_call(kernel, out_shape=[jax.ShapeDtypeStruct((512, 128), bf16)]...  50.1 us
    unnamed x2, local copies, waits for them, and re-layouts  1.31 us

profile of v5, /device:TPU:1, one launch (start us, length us, event | category | flops | bytes accessed | tf_op | source)
XLA Modules:
  0.0 52.1 jit_solution(11051962825890876500)
XLA Ops:
  0.6 50.1 %shard_map.68 = (bf16[512,128]{1,0:T(8,128)(2,1)S(1)}, bf16[512,128]{1,0:T(8,128)(2,1)S(1)}) custom-call(bf16[64,2,16,128]{3,2,1,0:T(8,128)(2,1)} %bitcast.10, bf16[2,32,128]{2,1,0:T(8,128)(2,1)} %bitcast.11, s32[64]{0:T(128)} %occupied_hbm.1, s32[64,64]{1,0:T(8,128)} %map_hbm.1, s32[64]{0:T(128)} %partner_hbm.1), custom_call_target="tpu_custom_call" | custom-call | tf_op jit(solution)/shard_map/pallas_call | solution.py:340
  50.7 0.7 %copy.11 = bf16[1,64,1,2,4,128]{5,4,3,2,1,0:T(4,128)(2,1)} copy(bf16[1,64,1,2,4,128]{5,4,3,2,1,0:T(4,128)(2,1)S(1)} %bitcast.9) | data formatting | bytes 262144
  51.4 0.7 %copy.12 = bf16[1,64,1,2,4,128]{5,4,3,2,1,0:T(4,128)(2,1)} copy(bf16[1,64,1,2,4,128]{5,4,3,2,1,0:T(4,128)(2,1)S(1)} %bitcast.8) | data formatting | bytes 262144

commit v6 on v5

--- a/solution.py
+++ b/solution.py
@@ -59,7 +59,8 @@
     z = zh * 8 + zl
     mine = x == y
     slot_me = 2 * zl + c
-    first_zl = (zl + (y - x + 4) % 4) % 8
+    offset = (y - x + 4) % 4
+    first_zl = (zl + offset + 4 * (offset // 3)) % 8
     second_zl = (first_zl + 4) % 8
 
     loads = [
@@ -133,12 +134,15 @@
 
     lax.fori_loop(1, 16, tell_ring, 0, unroll=True)
 
+    def plane_at(i, sign=1):
+        return (zl + sign * ((i + 1) // 2) * (2 * (i % 2) - 1) + 8) % 8
+
     def rows_from(jp, source):
         start = pl.multiple_of(zh * 64 + source * 16, 16)
         return work.at[jp, :, :, :, pl.ds(start, 16), :]
 
     def block_copy(i, d, source, target):
-        jp = (zl + i) % 8
+        jp = plane_at(i)
         return pltpu.make_async_remote_copy(
             src_ref=stage.at[target, jp],
             dst_ref=rows_from(jp, source),
@@ -149,7 +153,7 @@
         )
 
     def self_copy(i):
-        jp = (zl + i) % 8
+        jp = plane_at(i)
         return pltpu.make_async_copy(stage.at[y, jp], rows_from(jp, y), block_recv.at[i, 0])
 
     def trial_copy(slot, pb, vert, source=None):
@@ -178,8 +182,6 @@
         there = (z - d + 16) % 16
         trial_copy(slot_me, (there % 8) * 8 + x * 2 + c, (there // 8) * 4 + y, masked).start()
 
-    offset = (y - x + 4) % 4
-
     @pl.when(mine)
     def _():
         forward(zl)
@@ -204,7 +206,7 @@
     low = lax.broadcasted_iota(jnp.int32, (8, 128), 0) < 4
 
     def terms(i, carry):
-        jp = (zl + i) % 8
+        jp = plane_at(i)
 
 
         self_copy(i).wait()
@@ -287,9 +289,10 @@
         return code.astype(jnp.float32) * unit_of(last)
 
     def decode(o, carry):
-        start = pl.multiple_of((zl - o + 8) % 8 * 8, 8)
+        plane = plane_at(o, -1)
+        start = pl.multiple_of(plane * 8, 8)
         part = incoming.at[:, pl.ds(start, 8)]
-        pltpu.make_async_copy(part, part, term_recv.at[(zl - o + 8) % 8]).wait()
+        pltpu.make_async_copy(part, part, term_recv.at[plane]).wait()
 
         def one(n, carry):
             q = start + n

time: 52.2 us -> 51.3 us (0.983)
  Pallas kernels: 50.1 us -> 49.2 us
    pallas_call x1, Pallas kernels: 50.1 us -> 49.2 us  [local(): pl.pallas_call(kernel, out_shape=[jax.ShapeDtypeStruct((512, 128), bf16)]...]
where the time goes in v6:
time: 51.3 us; the launch traced here: 51.1 us
  Pallas kernels  49.2 us (96%)
  local copies, waits for them, and re-layouts  1.31 us (3%)
  between operations  0.64 us (1%)
    pallas_call x1, Pallas kernels, local(): pl.pallas_call(kernel, out_shape=[jax.ShapeDtypeStruct((512, 128), bf16)]...  49.2 us
    unnamed x2, local copies, waits for them, and re-layouts  1.31 us

profile of v6, /device:TPU:1, one launch (start us, length us, event | category | flops | bytes accessed | tf_op | source)
XLA Modules:
  0.0 51.1 jit_solution(11474495758658777005)
XLA Ops:
  0.6 49.2 %shard_map.68 = (bf16[512,128]{1,0:T(8,128)(2,1)S(1)}, bf16[512,128]{1,0:T(8,128)(2,1)S(1)}) custom-call(bf16[64,2,16,128]{3,2,1,0:T(8,128)(2,1)} %bitcast.10, bf16[2,32,128]{2,1,0:T(8,128)(2,1)} %bitcast.11, s32[64]{0:T(128)} %occupied_hbm.1, s32[64,64]{1,0:T(8,128)} %map_hbm.1, s32[64]{0:T(128)} %partner_hbm.1), custom_call_target="tpu_custom_call" | custom-call | tf_op jit(solution)/shard_map/pallas_call | solution.py:343
  49.8 0.7 %copy.11 = bf16[1,64,1,2,4,128]{5,4,3,2,1,0:T(4,128)(2,1)} copy(bf16[1,64,1,2,4,128]{5,4,3,2,1,0:T(4,128)(2,1)S(1)} %bitcast.9) | data formatting | bytes 262144
  50.5 0.7 %copy.12 = bf16[1,64,1,2,4,128]{5,4,3,2,1,0:T(4,128)(2,1)} copy(bf16[1,64,1,2,4,128]{5,4,3,2,1,0:T(4,128)(2,1)S(1)} %bitcast.8) | data formatting | bytes 262144

commit v7 on v6

--- a/solution.py
+++ b/solution.py
@@ -86,8 +86,11 @@
         greet(zl * 8 + ((x + i // 8) % 4) * 2 + (c + i) % 2, zh * 4 + (y + i // 2) % 4)
         return carry
 
-    lax.fori_loop(1, 16, greet_ring, 0, unroll=True)
-    lax.fori_loop(1, 32, greet_plane, 0, unroll=True)
+    for n, i in enumerate((8, 7, 9, 6, 10, 5, 11, 4, 12, 3, 13, 2, 14, 1, 15)):
+        greet_ring(i, 0)
+        greet_plane(2 * n + 1, 0)
+        greet_plane(2 * n + 2, 0)
+    greet_plane(31, 0)
 
     away = pl.multiple_of((1 - zh) * 64, 64)
 
@@ -132,7 +135,8 @@
         )
         return carry
 
-    lax.fori_loop(1, 16, tell_ring, 0, unroll=True)
+    for i in (8, 7, 9, 6, 10, 5, 11, 4, 12, 3, 13, 2, 14, 1, 15):
+        tell_ring(i, 0)
 
     def plane_at(i, sign=1):
         return (zl + sign * ((i + 1) // 2) * (2 * (i % 2) - 1) + 8) % 8
@@ -199,15 +203,16 @@
         forward(first_zl)
 
 
-    trial_copy(2 * second_zl + c, me, v).wait_recv()
-    forward(second_zl)
-
     here = pl.multiple_of(zh * 64, 64)
     low = lax.broadcasted_iota(jnp.int32, (8, 128), 0) < 4
 
     def terms(i, carry):
         jp = plane_at(i)
 
+        @pl.when(i == 2)
+        def _():
+            trial_copy(2 * second_zl + c, me, v).wait_recv()
+            forward(second_zl)
 
         self_copy(i).wait()
         for d in range(1, 4):
@@ -310,9 +315,9 @@
 
     def close(i, carry):
         results = [finish(2 * i), finish(2 * i + 1)]
-        start = pl.multiple_of(i * 16, 16)
-        plus_ref[pl.ds(start, 16), :] = jnp.concatenate([r[0] for r in results], axis=0).astype(jnp.bfloat16)
-        minus_ref[pl.ds(start, 16), :] = jnp.concatenate([r[1] for r in results], axis=0).astype(jnp.bfloat16)
+        for ref, n in ((plus_ref, 0), (minus_ref, 1)):
+            both = jnp.concatenate([r[n] for r in results], axis=0)
+            ref[pl.ds(4 * i, 4)] = both.reshape(4, 4, 128).astype(jnp.bfloat16)
         return carry
 
     lax.fori_loop(0, 32, close, 0, unroll=4)
@@ -333,6 +338,17 @@
     @pl.when(jnp.logical_not(mine))
     def _():
         pltpu.make_async_copy(outgoing, outgoing, term_send).wait()
+
+
+def deliver(plus_ref, minus_ref, plus_out, minus_out, sems):
+    copies = [
+        pltpu.make_async_copy(plus_ref, plus_out, sems.at[0]),
+        pltpu.make_async_copy(minus_ref, minus_out, sems.at[1]),
+    ]
+    for copy in copies:
+        copy.start()
+    for copy in copies:
+        copy.wait()
 
 
 def local(cholesky, trial_rows, occupied, kpoint_map, partner):
@@ -342,7 +358,7 @@
     bf16, i32 = jnp.bfloat16, jnp.int32
     plus, minus = pl.pallas_call(
         kernel,
-        out_shape=[jax.ShapeDtypeStruct((512, 128), bf16)] * 2,
+        out_shape=[jax.ShapeDtypeStruct((128, 4, 128), bf16)] * 2,
         in_specs=[pl.BlockSpec(memory_space=pl.ANY)] * 5,
         out_specs=[vmem, vmem],
         scratch_shapes=[
@@ -372,6 +388,15 @@
             collective_id=0, has_side_effects=True, vmem_limit_bytes=32 * 2**20
         ),
     )(*[pltpu.with_memory_space_constraint(a, pltpu.HBM) for a in (blocks, trial, occupied, kpoint_map, partner)])
+    anywhere = pl.BlockSpec(memory_space=pltpu.HBM)
+    plus, minus = pl.pallas_call(
+        deliver,
+        out_shape=[jax.ShapeDtypeStruct((128, 4, 128), bf16)] * 2,
+        in_specs=[vmem, vmem],
+        out_specs=[anywhere, anywhere],
+        scratch_shapes=[pltpu.SemaphoreType.DMA((2,))],
+        compiler_params=pltpu.CompilerParams(vmem_limit_bytes=32 * 2**20),
+    )(plus, minus)
     shape = (1, 64, 1, 2, 4, 128)
     return plus.reshape(shape), minus.reshape(shape)
 

time: 51.3 us -> 50.4 us (0.982)
  local copies, waits for them, and re-layouts: 1.31 us -> 0 us
    unnamed x2 -> x0, local copies, waits for them, and re-layouts: 1.31 us -> none
    pallas_call x1 -> x2, Pallas kernels: 49.2 us -> 49.6 us  [the longest x1 48.9 us: local(): pl.pallas_call(kernel, out_shape=[jax.ShapeDtypeStruct((128, 4, 128), bf1...]
where the time goes in v7:
time: 50.4 us; the launch traced here: 50.2 us
  Pallas kernels  49.6 us (98%)
  between operations  0.64 us (1%)
    pallas_call x1, Pallas kernels, local(): pl.pallas_call(kernel, out_shape=[jax.ShapeDtypeStruct((128, 4, 128), bf1...  48.9 us

profile of v7, /device:TPU:1, one launch (start us, length us, event | category | flops | bytes accessed | tf_op | source)
XLA Modules:
  0.0 50.2 jit_solution(15867601470814095041)
XLA Ops:
  0.6 48.9 %shard_map.68 = (bf16[128,4,128]{2,1,0:T(4,128)(2,1)S(1)}, bf16[128,4,128]{2,1,0:T(4,128)(2,1)S(1)}) custom-call(bf16[64,2,16,128]{3,2,1,0:T(8,128)(2,1)} %bitcast.8, bf16[2,32,128]{2,1,0:T(8,128)(2,1)} %bitcast.9, s32[64]{0:T(128)} %occupied_hbm.1, s32[64,64]{1,0:T(8,128)} %map_hbm.1, s32[64]{0:T(128)} %partner_hbm.1), custom_call_target="tpu_custom_call" | custom-call | tf_op jit(solution)/shard_map/pallas_call | solution.py:359
  49.5 0.7 %shard_map.69 = (bf16[128,4,128]{2,1,0:T(4,128)(2,1)}, bf16[128,4,128]{2,1,0:T(4,128)(2,1)}) custom-call(bf16[128,4,128]{2,1,0:T(4,128)(2,1)S(1)} %get-tuple-element.6.plus_ref, bf16[128,4,128]{2,1,0:T(4,128)(2,1)S(1)} %get-tuple-element.7.minus_ref), custom_call_target="tpu_custom_call" | custom-call | tf_op jit(solution)/shard_map/pallas_call | solution.py:392

commit v8 on v7

--- a/solution.py
+++ b/solution.py
@@ -50,8 +50,8 @@
 
 def kernel(
     blocks_hbm, trial_hbm, occupied_hbm, map_hbm, partner_hbm, plus_ref, minus_ref,
-    blocks, trial_ref, masked, occupied, kpoint_map, partner, stage, work, trials, outgoing, incoming, own_terms, mirror_terms,
-    plane_in, load_sem, block_send, block_recv, trial_send, trial_recv, term_send, term_recv,
+    blocks, trial_ref, masked, occupied, kpoint_map, partner, stage, work, trials, outgoing, incoming, relay, own_terms, mirror_terms,
+    plane_in, relay_send, relay_recv, load_sem, block_send, block_recv, trial_send, trial_recv, term_send, term_recv,
 ):
     me, v = lax.axis_index("pb"), lax.axis_index("vert")
     zl, x, c = me // 8, (me // 2) % 4, me % 2
@@ -206,13 +206,53 @@
     here = pl.multiple_of(zh * 64, 64)
     low = lax.broadcasted_iota(jnp.int32, (8, 128), 0) < 4
 
-    def terms(i, carry):
+    def send_term(source, k, w, sender_zh):
+        own_tile = (k == me) & (w == v)
+        target = incoming.at[sender_zh, me]
+
+        @pl.when(own_tile)
+        def _():
+            pltpu.make_async_copy(source, target, term_recv.at[zl]).start()
+
+        @pl.when(jnp.logical_not(own_tile))
+        def _():
+            pltpu.make_async_remote_copy(
+                src_ref=source,
+                dst_ref=target,
+                send_sem=term_send,
+                recv_sem=term_recv.at[zl],
+                device_id=(k, w),
+                device_id_type=MESH,
+            ).start()
+
+    def relay_copy(slot, cp):
+        return pltpu.make_async_remote_copy(
+            src_ref=outgoing.at[slot, pl.ds((1 - zh) * 4, 4)],
+            dst_ref=relay.at[cp],
+            send_sem=relay_send,
+            recv_sem=relay_recv,
+            device_id=(me, (1 - zh) * 4 + y),
+            device_id_type=MESH,
+        )
+
+    def hand_on():
+        pltpu.make_async_copy(relay, relay, relay_recv).wait()
+        for cp in range(2):
+            for n in range(4):
+                send_term(relay.at[cp, n], kpoint(zl, cp, y, zl), zh * 4 + n, 1 - zh)
+
+    def terms(first, i, carry):
         jp = plane_at(i)
-
-        @pl.when(i == 2)
-        def _():
-            trial_copy(2 * second_zl + c, me, v).wait_recv()
-            forward(second_zl)
+        if not first:
+
+            @pl.when(i == 2)
+            def _():
+                trial_copy(2 * second_zl + c, me, v).wait_recv()
+                forward(second_zl)
+
+            @pl.when(i == 4)
+            def _():
+                hand_on()
 
         self_copy(i).wait()
         for d in range(1, 4):
@@ -240,33 +280,24 @@
             k = kpoint(jp, cp, y, zl)
             for w in range(8):
                 outgoing[slot, w] = messages[w][:7]
+            if first:
+                for n in range(4):
+                    send_term(outgoing.at[slot, zh * 4 + n], k, zh * 4 + n, zh)
+                relay_copy(slot, cp).start()
+                continue
             if cp == 0:
 
-                @pl.when(i == 0)
+                @pl.when(i == 1)
                 def _():
                     pl.semaphore_wait(plane_in, 15)
 
             for w in range(8):
-                own_tile = (k == me) & (w == v)
-
-                @pl.when(own_tile)
-                def _():
-                    pltpu.make_async_copy(outgoing.at[slot, w], incoming.at[zh, me], term_recv.at[zl]).start()
-
-                @pl.when(jnp.logical_not(own_tile))
-                def _():
-                    pltpu.make_async_remote_copy(
-                        src_ref=outgoing.at[slot, w],
-                        dst_ref=incoming.at[zh, me],
-                        send_sem=term_send,
-                        recv_sem=term_recv.at[zl],
-                        device_id=(k, w),
-                        device_id_type=MESH,
-                    ).start()
-
-        return carry
-
-    lax.fori_loop(0, 8, terms, 0)
+                send_term(outgoing.at[slot, w], k, w, zh)
+
+        return carry
+
+    terms(True, 0, 0)
+    lax.fori_loop(1, 8, functools.partial(terms, False), 0)
 
     lane = lax.broadcasted_iota(jnp.int32, (8, 128), 1) < 64
     stay = low == lane
@@ -322,6 +353,7 @@
 
     lax.fori_loop(0, 32, close, 0, unroll=4)
 
+    pltpu.make_async_copy(relay, relay, relay_send).wait()
     pltpu.make_async_copy(stage.at[0:3], stage.at[0:3], block_send).wait()
 
     pltpu.make_async_copy(trials.at[0:15], trials.at[0:15], trial_send).wait()
@@ -333,7 +365,7 @@
     @pl.when(mine)
     def _():
         pltpu.make_async_copy(outgoing.at[0:15], outgoing.at[0:15], term_send).wait()
-        pltpu.make_async_copy(outgoing.at[0, 0:7], outgoing.at[0, 0:7], term_send).wait()
+        pltpu.make_async_copy(outgoing.at[0, 0:6], outgoing.at[0, 0:6], term_send).wait()
 
     @pl.when(jnp.logical_not(mine))
     def _():
@@ -373,9 +405,12 @@
             pltpu.VMEM((16, 2, 32, 128), bf16),
             pltpu.VMEM((16, 8, 7, 128), i32),
             pltpu.VMEM((2, 64, 7, 128), i32),
+            pltpu.VMEM((2, 4, 7, 128), i32),
             pltpu.VMEM((64, 8, 128), jnp.float32),
             pltpu.VMEM((64, 8, 128), jnp.float32),
             pltpu.SemaphoreType.REGULAR,
+            pltpu.SemaphoreType.DMA,
+            pltpu.SemaphoreType.DMA,
             pltpu.SemaphoreType.DMA((5,)),
             pltpu.SemaphoreType.DMA,
             pltpu.SemaphoreType.DMA((8, 4)),

time: 50.4 us -> 49.7 us (0.986)
  Pallas kernels: 49.6 us -> 48.9 us
    pallas_call x1, Pallas kernels: 48.9 us -> 48.1 us  [local(): pl.pallas_call(kernel, out_shape=[jax.ShapeDtypeStruct((128, 4, 128), bf1...]
where the time goes in v8:
time: 49.7 us; the launch traced here: 49.5 us
  Pallas kernels  48.9 us (98%)
  between operations  0.64 us (1%)
    pallas_call x1, Pallas kernels, local(): pl.pallas_call(kernel, out_shape=[jax.ShapeDtypeStruct((128, 4, 128), bf1...  48.1 us

profile of v8, /device:TPU:1, one launch (start us, length us, event | category | flops | bytes accessed | tf_op | source)
XLA Modules:
  0.0 49.5 jit_solution(13504323295990679419)
XLA Ops:
  0.6 48.1 %shard_map.68 = (bf16[128,4,128]{2,1,0:T(4,128)(2,1)S(1)}, bf16[128,4,128]{2,1,0:T(4,128)(2,1)S(1)}) custom-call(bf16[64,2,16,128]{3,2,1,0:T(8,128)(2,1)} %bitcast.8, bf16[2,32,128]{2,1,0:T(8,128)(2,1)} %bitcast.9, s32[64]{0:T(128)} %occupied_hbm.1, s32[64,64]{1,0:T(8,128)} %map_hbm.1, s32[64]{0:T(128)} %partner_hbm.1), custom_call_target="tpu_custom_call" | custom-call | tf_op jit(solution)/shard_map/pallas_call | solution.py:391
  48.8 0.7 %shard_map.69 = (bf16[128,4,128]{2,1,0:T(4,128)(2,1)}, bf16[128,4,128]{2,1,0:T(4,128)(2,1)}) custom-call(bf16[128,4,128]{2,1,0:T(4,128)(2,1)S(1)} %get-tuple-element.6.plus_ref, bf16[128,4,128]{2,1,0:T(4,128)(2,1)S(1)} %get-tuple-element.7.minus_ref), custom_call_target="tpu_custom_call" | custom-call | tf_op jit(solution)/shard_map/pallas_call | solution.py:427

commit v9 on v8

--- a/solution.py
+++ b/solution.py
@@ -50,8 +50,8 @@
 
 def kernel(
     blocks_hbm, trial_hbm, occupied_hbm, map_hbm, partner_hbm, plus_ref, minus_ref,
-    blocks, trial_ref, masked, occupied, kpoint_map, partner, stage, work, trials, outgoing, incoming, relay, own_terms, mirror_terms,
-    plane_in, relay_send, relay_recv, load_sem, block_send, block_recv, trial_send, trial_recv, term_send, term_recv,
+    blocks, trial_ref, masked, occupied, kpoint_map, partner, stage, work, trials, outgoing, incoming, relay, relayed, own_terms, mirror_terms,
+    plane_in, relay_send, relay_recv, next_send, next_recv, load_sem, block_send, block_recv, trial_send, trial_recv, term_send, term_recv,
 ):
     me, v = lax.axis_index("pb"), lax.axis_index("vert")
     zl, x, c = me // 8, (me // 2) % 4, me % 2
@@ -206,13 +206,13 @@
     here = pl.multiple_of(zh * 64, 64)
     low = lax.broadcasted_iota(jnp.int32, (8, 128), 0) < 4
 
-    def send_term(source, k, w, sender_zh):
+    def send_term(source, k, w, sender_zh, sender_zl):
         own_tile = (k == me) & (w == v)
-        target = incoming.at[sender_zh, me]
+        target = incoming.at[sender_zh, sender_zl * 8 + x * 2 + c]
 
         @pl.when(own_tile)
         def _():
-            pltpu.make_async_copy(source, target, term_recv.at[zl]).start()
+            pltpu.make_async_copy(source, target, term_recv.at[sender_zl]).start()
 
         @pl.when(jnp.logical_not(own_tile))
         def _():
@@ -220,7 +220,7 @@
                 src_ref=source,
                 dst_ref=target,
                 send_sem=term_send,
-                recv_sem=term_recv.at[zl],
+                recv_sem=term_recv.at[sender_zl],
                 device_id=(k, w),
                 device_id_type=MESH,
             ).start()
@@ -239,11 +239,29 @@
         pltpu.make_async_copy(relay, relay, relay_recv).wait()
         for cp in range(2):
             for n in range(4):
-                send_term(relay.at[cp, n], kpoint(zl, cp, y, zl), zh * 4 + n, 1 - zh)
-
-    def terms(first, i, carry):
+                send_term(relay.at[cp, n], kpoint(zl, cp, y, zl), zh * 4 + n, 1 - zh, zl)
+
+    def relay_next(slot, cp, half):
+        return pltpu.make_async_remote_copy(
+            src_ref=outgoing.at[slot, pl.ds(half * 4, 4)],
+            dst_ref=relayed.at[zh, cp],
+            send_sem=next_send,
+            recv_sem=next_recv,
+            device_id=((zl + 1) % 8 * 8 + x * 2 + c, half * 4 + y),
+            device_id_type=MESH,
+        )
+
+    def hand_on_next():
+        pltpu.make_async_copy(relayed, relayed, next_recv).wait()
+        before = (zl + 7) % 8
+        for h in range(2):
+            for cp in range(2):
+                for n in range(4):
+                    send_term(relayed.at[h, cp, n], kpoint(zl, cp, y, before), zh * 4 + n, h, before)
+
+    def terms(early, i, carry):
         jp = plane_at(i)
-        if not first:
+        if not early:
 
             @pl.when(i == 2)
             def _():
@@ -253,6 +271,10 @@
             @pl.when(i == 4)
             def _():
                 hand_on()
+
+            @pl.when(i == 5)
+            def _():
+                hand_on_next()
 
         self_copy(i).wait()
         for d in range(1, 4):
@@ -280,24 +302,29 @@
             k = kpoint(jp, cp, y, zl)
             for w in range(8):
                 outgoing[slot, w] = messages[w][:7]
-            if first:
+            if early and i == 1:
+                for half in range(2):
+                    relay_next(slot, cp, half).start()
+                continue
+            if early:
                 for n in range(4):
-                    send_term(outgoing.at[slot, zh * 4 + n], k, zh * 4 + n, zh)
+                    send_term(outgoing.at[slot, zh * 4 + n], k, zh * 4 + n, zh, zl)
                 relay_copy(slot, cp).start()
                 continue
             if cp == 0:
 
-                @pl.when(i == 1)
+                @pl.when(i == 2)
                 def _():
                     pl.semaphore_wait(plane_in, 15)
 
             for w in range(8):
-                send_term(outgoing.at[slot, w], k, w, zh)
+                send_term(outgoing.at[slot, w], k, w, zh, zl)
 
         return carry
 
     terms(True, 0, 0)
-    lax.fori_loop(1, 8, functools.partial(terms, False), 0)
+    terms(True, 1, 0)
+    lax.fori_loop(2, 8, functools.partial(terms, False), 0)
 
     lane = lax.broadcasted_iota(jnp.int32, (8, 128), 1) < 64
     stay = low == lane
@@ -354,6 +381,7 @@
     lax.fori_loop(0, 32, close, 0, unroll=4)
 
     pltpu.make_async_copy(relay, relay, relay_send).wait()
+    pltpu.make_async_copy(relayed, relayed, next_send).wait()
     pltpu.make_async_copy(stage.at[0:3], stage.at[0:3], block_send).wait()
 
     pltpu.make_async_copy(trials.at[0:15], trials.at[0:15], trial_send).wait()
@@ -362,12 +390,12 @@
     def _():
         pltpu.make_async_copy(trials.at[0], trials.at[0], trial_send).wait()
 
-    @pl.when(mine)
+    @pl.when(offset < 2)
     def _():
         pltpu.make_async_copy(outgoing.at[0:15], outgoing.at[0:15], term_send).wait()
         pltpu.make_async_copy(outgoing.at[0, 0:6], outgoing.at[0, 0:6], term_send).wait()
 
-    @pl.when(jnp.logical_not(mine))
+    @pl.when(offset >= 2)
     def _():
         pltpu.make_async_copy(outgoing, outgoing, term_send).wait()
 
@@ -406,9 +434,12 @@
             pltpu.VMEM((16, 8, 7, 128), i32),
             pltpu.VMEM((2, 64, 7, 128), i32),
             pltpu.VMEM((2, 4, 7, 128), i32),
+            pltpu.VMEM((2, 2, 4, 7, 128), i32),
             pltpu.VMEM((64, 8, 128), jnp.float32),
             pltpu.VMEM((64, 8, 128), jnp.float32),
             pltpu.SemaphoreType.REGULAR,
+            pltpu.SemaphoreType.DMA,
+            pltpu.SemaphoreType.DMA,
             pltpu.SemaphoreType.DMA,
             pltpu.SemaphoreType.DMA,
             pltpu.SemaphoreType.DMA((5,)),

time: 49.7 us -> 49 us (0.986)
  Pallas kernels: 48.9 us -> 48.2 us
    pallas_call x1, Pallas kernels: 48.1 us -> 47.5 us  [local(): pl.pallas_call(kernel, out_shape=[jax.ShapeDtypeStruct((128, 4, 128), bf1...]
where the time goes in v9:
time: 49 us; the launch traced here: 48.9 us
  Pallas kernels  48.2 us (98%)
  between operations  0.64 us (1%)
    pallas_call x1, Pallas kernels, local(): pl.pallas_call(kernel, out_shape=[jax.ShapeDtypeStruct((128, 4, 128), bf1...  47.5 us

profile of v9, /device:TPU:1, one launch (start us, length us, event | category | flops | bytes accessed | tf_op | source)
XLA Modules:
  0.0 48.9 jit_solution(5396958073289899636)
XLA Ops:
  0.6 47.5 %shard_map.68 = (bf16[128,4,128]{2,1,0:T(4,128)(2,1)S(1)}, bf16[128,4,128]{2,1,0:T(4,128)(2,1)S(1)}) custom-call(bf16[64,2,16,128]{3,2,1,0:T(8,128)(2,1)} %bitcast.8, bf16[2,32,128]{2,1,0:T(8,128)(2,1)} %bitcast.9, s32[64]{0:T(128)} %occupied_hbm.1, s32[64,64]{1,0:T(8,128)} %map_hbm.1, s32[64]{0:T(128)} %partner_hbm.1), custom_call_target="tpu_custom_call" | custom-call | tf_op jit(solution)/shard_map/pallas_call | solution.py:419
  48.1 0.7 %shard_map.69 = (bf16[128,4,128]{2,1,0:T(4,128)(2,1)}, bf16[128,4,128]{2,1,0:T(4,128)(2,1)}) custom-call(bf16[128,4,128]{2,1,0:T(4,128)(2,1)S(1)} %get-tuple-element.6.plus_ref, bf16[128,4,128]{2,1,0:T(4,128)(2,1)S(1)} %get-tuple-element.7.minus_ref), custom_call_target="tpu_custom_call" | custom-call | tf_op jit(solution)/shard_map/pallas_call | solution.py:458

commit v10 on v9

--- a/solution.py
+++ b/solution.py
@@ -128,16 +128,6 @@
 
     pl.semaphore_wait(barrier, 46)
 
-    def tell_ring(i, carry):
-        there = (z + i) % 16
-        pl.semaphore_signal(
-            plane_in, inc=1, device_id=((there % 8) * 8 + x * 2 + c, (there // 8) * 4 + y), device_id_type=MESH
-        )
-        return carry
-
-    for i in (8, 7, 9, 6, 10, 5, 11, 4, 12, 3, 13, 2, 14, 1, 15):
-        tell_ring(i, 0)
-
     def plane_at(i, sign=1):
         return (zl + sign * ((i + 1) // 2) * (2 * (i % 2) - 1) + 8) % 8
 
@@ -180,8 +170,6 @@
             block_copy(i, d, y, (y + d) % 4).start()
         return carry
 
-    block_sends(0, 0)
-
     def trial_along(d):
         there = (z - d + 16) % 16
         trial_copy(slot_me, (there % 8) * 8 + x * 2 + c, (there // 8) * 4 + y, masked).start()
@@ -195,6 +183,18 @@
         trial_along(offset)
 
     trial_along(offset - 4)
+    def tell_ring(i, carry):
+        there = (z + i) % 16
+        pl.semaphore_signal(
+            plane_in, inc=1, device_id=((there % 8) * 8 + x * 2 + c, (there // 8) * 4 + y), device_id_type=MESH
+        )
+        return carry
+
+    for i in (8, 7, 9, 6, 10, 5, 11, 4, 12, 3, 13, 2, 14, 1, 15):
+        tell_ring(i, 0)
+
+    block_sends(0, 0)
+
     lax.fori_loop(1, 8, block_sends, 0, unroll=True)
 
     @pl.when(jnp.logical_not(mine))

time: 49 us -> 49.1 us (level)
  no operation moved by 1% of the time
where the time goes in v10:
time: 49.1 us; the launch traced here: 48.6 us
  Pallas kernels  48 us (98%)
  between operations  0.64 us (1%)
    pallas_call x1, Pallas kernels, local(): pl.pallas_call(kernel, out_shape=[jax.ShapeDtypeStruct((128, 4, 128), bf1...  47.3 us

profile of v10, /device:TPU:1, one launch (start us, length us, event | category | flops | bytes accessed | tf_op | source)
XLA Modules:
  0.0 48.6 jit_solution(3362859083795559926)
XLA Ops:
  0.6 47.3 %shard_map.68 = (bf16[128,4,128]{2,1,0:T(4,128)(2,1)S(1)}, bf16[128,4,128]{2,1,0:T(4,128)(2,1)S(1)}) custom-call(bf16[64,2,16,128]{3,2,1,0:T(8,128)(2,1)} %bitcast.8, bf16[2,32,128]{2,1,0:T(8,128)(2,1)} %bitcast.9, s32[64]{0:T(128)} %occupied_hbm.1, s32[64,64]{1,0:T(8,128)} %map_hbm.1, s32[64]{0:T(128)} %partner_hbm.1), custom_call_target="tpu_custom_call" | custom-call | tf_op jit(solution)/shard_map/pallas_call | solution.py:419
  47.9 0.7 %shard_map.69 = (bf16[128,4,128]{2,1,0:T(4,128)(2,1)}, bf16[128,4,128]{2,1,0:T(4,128)(2,1)}) custom-call(bf16[128,4,128]{2,1,0:T(4,128)(2,1)S(1)} %get-tuple-element.6.plus_ref, bf16[128,4,128]{2,1,0:T(4,128)(2,1)S(1)} %get-tuple-element.7.minus_ref), custom_call_target="tpu_custom_call" | custom-call | tf_op jit(solution)/shard_map/pallas_call | solution.py:458
